TPU v7x, 256 devices: a whole 4x4x8 slice. The times are simulated.
256 devices in a mesh: dp: 4 (over x_lo, core), sample: 8 (over y, x_hi), head: 8 (over z).
Axes of the slice: x: 4 (x_hi: 2, x_lo: 2; x = x_hi * 2 + x_lo), y: 4, z: 8, core: 2. Of those that a mesh axis runs over, the one named last changes fastest.
Arguments:
- prompt_latent: bfloat16 [4, 512, 512], P('dp', ('sample', 'head')), may hold values from -6 to 6
- prompt_rope: bfloat16 [4, 512, 64], P('dp', ('sample', 'head')), may hold values from -6 to 6
- comp_latent: bfloat16 [4, 8, 256, 512], P('dp', 'sample'), may hold values from -6 to 6
- comp_rope: bfloat16 [4, 8, 256, 64], P('dp', 'sample'), may hold values from -6 to 6
- query_nope: bfloat16 [4, 8, 256, 16384], P('dp', 'sample', None, 'head'), may hold values from -6 to 6
- query_rope: bfloat16 [4, 8, 256, 8192], P('dp', 'sample', None, 'head'), may hold values from -100 to 100
- grad_out: bfloat16 [4, 8, 256, 16384], P('dp', 'sample', None, 'head'), may hold values from -48 to 48
- lengths: int32 [4, 8], P('dp', 'sample'), may hold values from 32 to 256, as said below
- w_uk: bfloat16 [512, 16384], P(None, 'head'), may hold values from -0.25 to 0.25
- w_uv: bfloat16 [512, 16384], P(None, 'head'), may hold values from -0.25 to 0.25
Outputs:
- grad_latent: float32 [4, 512, 512], P('dp', ('sample', 'head'))
- grad_rope: float32 [4, 512, 64], P('dp', ('sample', 'head'))
- grad_w_uk: float32 [512, 16384], P(('dp', 'sample'), 'head')
- grad_w_uv: float32 [512, 16384], P(('dp', 'sample'), 'head')
Inputs may be any that keep to these rules, and one draw needn't show every extreme that they name: `lengths`: each prompt has one completion with all 256 slots live.
All inputs are finite; a program needn't handle non-finite values.
Results may differ from a plain program's by a relative error of at most 0.0097.
Values may be sent and summed in bfloat16 or wider, within the bound.
A program may use at most 128 MiB of HBM per device.

v0:
```python
import jax
import jax.numpy as jnp
from jax import lax
from jax.sharding import PartitionSpec as P

DR = 64
DH = 128


def attend(query_nope, query_rope, grad_out, all_keys, all_values, all_rope, length):
    row_count = query_nope.shape[0]
    key_count = all_keys.shape[0]
    prompt_count = key_count - row_count
    score_scale = 1.0 / (query_nope.shape[2] + query_rope.shape[2]) ** 0.5
    score = jnp.einsum("rhd,khd->hrk", query_nope, all_keys, preferred_element_type=jnp.float32)
    score = score + jnp.einsum(
        "rhd,kd->hrk", query_rope, all_rope, preferred_element_type=jnp.float32
    )
    score = score * score_scale
    row_index = jnp.arange(row_count, dtype=jnp.int32)[:, None]
    key_index = jnp.arange(key_count, dtype=jnp.int32)[None, :]
    visible = (key_index < prompt_count) | (key_index - prompt_count <= row_index)
    score = jnp.where(visible[None], score, -1e30)
    probs = jax.nn.softmax(score, axis=-1)
    probs_b = probs.astype(jnp.bfloat16)
    output = jnp.einsum("hrk,khd->rhd", probs_b, all_values, preferred_element_type=jnp.float32)
    live_rows = (jnp.arange(row_count, dtype=jnp.int32) < length)[:, None, None]
    cotangent = jnp.where(live_rows, grad_out, jnp.zeros_like(grad_out))
    row_delta = jnp.sum(cotangent.astype(jnp.float32) * output, axis=-1)
    dprob = jnp.einsum("rhd,khd->hrk", cotangent, all_values, preferred_element_type=jnp.float32)
    dscore = (probs * (dprob - row_delta.T[:, :, None])).astype(jnp.bfloat16)
    dkeys = (
        score_scale
        * jnp.einsum("hrk,rhd->khd", dscore, query_nope, preferred_element_type=jnp.float32)
    ).astype(jnp.bfloat16)
    drope = score_scale * jnp.einsum(
        "hrk,rhd->kd", dscore, query_rope, preferred_element_type=jnp.float32
    )
    dvalues = jnp.einsum(
        "hrk,rhd->khd", probs_b, cotangent, preferred_element_type=jnp.float32
    ).astype(jnp.bfloat16)
    return (dkeys, dvalues, drope)


def left_product(latent_cols, grads):
    return lax.dot_general(
        latent_cols, grads, (((0,), (0,)), ((), ())), preferred_element_type=jnp.float32
    )


def local(
    prompt_latent,
    prompt_rope,
    comp_latent,
    comp_rope,
    query_nope,
    query_rope,
    grad_out,
    lengths,
    w_uk,
    w_uv,
):
    head_width = w_uk.shape[1]
    local_heads = head_width // DH
    comp_rows = comp_latent[0, 0]
    comp_keyrope = comp_rope[0, 0]
    row_count = comp_rows.shape[0]
    queries = query_nope[0, 0].reshape(row_count, local_heads, DH)
    query_pos = query_rope[0, 0].reshape(row_count, local_heads, DR)
    cotangent = grad_out[0, 0].reshape(row_count, local_heads, DH)
    length = lengths[0, 0]
    comp_keys = jnp.dot(comp_rows, w_uk, preferred_element_type=jnp.float32).astype(jnp.bfloat16)
    comp_values = jnp.dot(comp_rows, w_uv, preferred_element_type=jnp.float32).astype(jnp.bfloat16)
    whole_latent, whole_rope = (
        lax.all_gather(prompt_latent, ("sample", "head"), axis=1, tiled=True),
        lax.all_gather(prompt_rope, ("sample", "head"), axis=1, tiled=True),
    )
    latent_rows = whole_latent[0]
    rope_rows = whole_rope[0]
    prompt_keys = jnp.dot(latent_rows, w_uk, preferred_element_type=jnp.float32).astype(
        jnp.bfloat16
    )
    prompt_values = jnp.dot(latent_rows, w_uv, preferred_element_type=jnp.float32).astype(
        jnp.bfloat16
    )
    prompt_count = prompt_keys.shape[0]
    all_keys = jnp.concatenate([prompt_keys, comp_keys], 0).reshape(
        prompt_count + row_count, local_heads, DH
    )
    all_values = jnp.concatenate([prompt_values, comp_values], 0).reshape(
        prompt_count + row_count, local_heads, DH
    )
    all_rope = jnp.concatenate([rope_rows, comp_keyrope], 0)
    dkeys, dvalues, drope = attend(
        queries, query_pos, cotangent, all_keys, all_values, all_rope, length
    )
    dkeys = dkeys.reshape(prompt_count + row_count, head_width)
    dvalues = dvalues.reshape(prompt_count + row_count, head_width)
    prompt_grads = jnp.concatenate([dkeys[:prompt_count], dvalues[:prompt_count]], 1)
    comp_grads = jnp.concatenate([dkeys[prompt_count:], dvalues[prompt_count:]], 1)
    dims_right = (((1,), (1,)), ((), ()))
    latent_term = lax.dot_general(
        dkeys[:prompt_count], w_uk, dims_right, preferred_element_type=jnp.float32
    )
    latent_term = latent_term + lax.dot_general(
        dvalues[:prompt_count], w_uv, dims_right, preferred_element_type=jnp.float32
    )
    grad_latent, grad_rope = (
        lax.psum_scatter(latent_term, ("sample", "head"), scatter_dimension=0, tiled=True),
        lax.psum_scatter(drope[:prompt_count], ("sample", "head"), scatter_dimension=0, tiled=True),
    )
    weights = lax.psum_scatter(
        left_product(latent_rows, prompt_grads) + left_product(comp_rows, comp_grads),
        ("dp", "sample"),
        scatter_dimension=0,
        tiled=True,
    )
    return (grad_latent[None], grad_rope[None], weights[:, :head_width], weights[:, head_width:])


def solution(mesh):
    in_specs = (
        P("dp", ("sample", "head"), None),
        P("dp", ("sample", "head"), None),
        P("dp", "sample", None, None),
        P("dp", "sample", None, None),
        P("dp", "sample", None, "head"),
        P("dp", "sample", None, "head"),
        P("dp", "sample", None, "head"),
        P("dp", "sample"),
        P(None, "head"),
        P(None, "head"),
    )
    out_specs = (
        P("dp", ("sample", "head"), None),
        P("dp", ("sample", "head"), None),
        P(("dp", "sample"), "head"),
        P(("dp", "sample"), "head"),
    )
    return jax.shard_map(local, mesh=mesh, in_specs=in_specs, out_specs=out_specs, check_vma=False)
```

profile of v0, /device:TPU:2, one launch (start us, length us, event | category | flops | bytes accessed | tf_op | source)
XLA Modules:
  0.0 1099.4 jit_solution(676256511329315098)
XLA Ops:
  8.0 0.0 copy-start
  8.0 0.0 all-reduce.3.cloned.1.call-start
  8.1 186.9 %all_gather.6 = bf16[1,512,512]{2,1,0:T(8,128)(2,1)S(1)} all-gather(bf16[1,8,512]{2,1,0:T(8,128)(2,1)} %param.10), channel_id=1, replica_groups=mesh['dp'=4,'sample'=8,'head'=8] {'sample','head'}, dimensions={1}, use_global_device_ids=true | all-gather | bytes 532480 | tf_op jit(solution)/shard_map/all_gather | solution.py:75
  195.0 2.6 convolution_convert_fusion.1
  197.6 1.7 convolution_convert_fusion.3
  199.3 2.6 convolution_convert_fusion
  201.9 1.7 convolution_convert_fusion.2
  203.6 1.5 copy.78
  205.1 2.1 copy.52
  207.2 174.5 %all_gather.7 = bf16[1,512,64]{2,1,0:T(8,128)(2,1)S(1)} all-gather(bf16[1,8,64]{2,1,0:T(8,128)(2,1)S(1)} %copy-done.16), channel_id=1, replica_groups=mesh['dp'=4,'sample'=8,'head'=8] {'sample','head'}, dimensions={1}, use_global_device_ids=true | all-gather | bytes 66560 | tf_op jit(solution)/shard_map/all_gather | solution.py:76
  381.7 0.7 copy.51
  382.4 4.0 pad_maximum_fusion
  386.4 4.7 copy.79
  391.2 2.3 copy.53
  394.1 0.9 fusion.16
  395.0 8.3 fusion.9
  403.3 0.0 copy-done.15
  403.3 13.6 %fusion.33 = (f32[16,256]{1,0:T(8,128)S(1)}, f32[16,256,768]{1,2,0:T(8,128)}) fusion(f32[16,768,256]{2,1,0:T(8,128)} %fusion.9, pred[256,768]{0,1:T(8,128)(4,1)} %fusion.16, bf16[256,16,64]{0,2,1:T(8,128)(2,1)} %bitcast.92, bf16[256,64]{0,1:T(8,128)(2,1)S(1)} %bitcast.104, bf16[512,64]{0,1:T(8,128)(2,1)S(1)} %bitcast.103), kind=kOutput, calls=%fused_computation.57 | convolution fusion | flops 418579200 | bytes 26001408 | tf_op jit(solution)/shard_map/sub | solution.py:24
  416.9 8.6 fusion.3
  425.5 4.8 fusion.15
  430.3 8.1 multiply_convert_fusion
  438.4 3.4 convolution_bitcast_fusion
  441.9 0.7 slice_multiply_fusion
  442.5 0.0 all-reduce.3.cloned.1.call-update
  442.6 0.3 reduce-scatter.8.cloned.1.call-start
  442.8 5.1 fusion.8
  447.9 6.1 convert_bitcast_fusion
  454.0 0.2 slice.46
  454.2 0.2 slice.47
  454.4 1.2 copy-done.3
  455.7 0.7 copy-done.7
  456.3 2.4 fusion.4
  458.7 4.5 add_bitcast_fusion
  463.2 9.0 copy.74
  472.2 0.0 reduce-scatter.8.cloned.1.call-update
  472.2 0.0 reduce-scatter.6.cloned.1.call-start
  472.3 0.0 copy-start.9
  472.3 0.0 copy-start.11
  472.3 3.0 fusion.34
  475.3 0.0 copy-done.9
  475.3 0.0 copy-start.17
  475.4 2.4 convolution_add_fusion
  477.7 0.0 reduce-scatter.6.cloned.1.call-update
  477.8 0.6 dynamic-slice
  479.0 609.8 %all-reduce.3.cloned.1.call-done = f32[512,64]{0,1:T(8,128)} async-done(((f32[512,64]{0,1:T(8,128)}), f32[512,64]{0,1:T(8,128)}) %all-reduce.3.cloned.1.call-update) | async-done | bytes 131088
  1088.8 0.8 dynamic-slice_bitcast_fusion
  1089.7 0.7 copy.63
  1090.3 1.7 fusion.32
  (37 shorter events, 0.1 us)
Async XLA Ops:
  8.0 187.0 %copy-start = (bf16[512,2048]{1,0:T(8,128)(2,1)S(1)}, bf16[512,2048]{1,0:T(8,128)(2,1)}, u32[]{:S(2)}) copy-start(bf16[512,2048]{1,0:T(8,128)(2,1)} %param.18) | copy-start | bytes 6291460
  8.0 1080.8 %all-reduce.3.cloned.1.call-start = ((), (), s32[]{:S(2)}) async-start(), calls=%async_computation.4 | async-start | bytes 262144
  195.0 4.3 copy-start.12
  195.0 2.6 copy-start.6
  197.6 1.7 copy-start.10
  201.9 5.3 copy-start.16
  395.0 8.3 copy-start.14
  395.0 8.3 copy-start.15
  416.9 8.6 copy-start.4
  438.4 3.4 copy-start.1
  442.6 647.8 %reduce-scatter.8.cloned.1.call-start = ((), (), s32[]{:S(2)}) async-start(), calls=%async_computation.3 | async-start | bytes 8650752
  442.8 5.1 copy-start.5
  447.9 6.3 copy-start.2
  454.0 1.6 copy-start.3
  454.2 2.1 copy-start.7
  454.2 2.1 copy-start.13
  455.7 3.1 copy-start.8
  456.3 2.4 slice-start
  456.3 2.4 slice-start.1
  472.2 619.8 %reduce-scatter.6.cloned.1.call-start = ((), (), s32[]{:S(2)}) async-start(), calls=%async_computation.2 | async-start | bytes 1064960 | tf_op jit(solution)/shard_map/reduce_scatter | solution.py:109
  472.3 3.1 copy-start.9
  472.3 3.1 copy-start.11
  475.3 2.4 copy-start.17
Sparse Core Ops, SparseCore 0:
  442.7 646.1 all-reduce.2
Sparse Core Ops, SparseCore 1:
  472.3 194.2 reduce-scatter.7
  669.5 380.0 reduce-scatter.5
where the time goes:
time: 1100 us
  waiting for transfers between devices  610 us (55%)
  blocking collectives  361 us (33%)
  matrix products  70.2 us (6%)
  local copies, waits for them, and re-layouts  26.3 us (2%)
  between operations  17.1 us (2%)
  other arithmetic  14.2 us (1%)
    unnamed x5, waiting for transfers between devices  610 us
    all_gather x1, blocking collectives, local(): lax.all_gather(prompt_latent, ('sample', 'head'), axis=1, tiled=True)  187 us
    all_gather x1, blocking collectives, local(): lax.all_gather(prompt_rope, ('sample', 'head'), axis=1, tiled=True)  175 us
  transfers between devices with their start and end apart: 3, of which 1 were waited for; matrix products, arithmetic and copies ran while one was open for 3% of the time, Pallas kernels for 0%

commit v1 on v0

v1 whole, which is shorter than its diff:
```python
import math

import jax
import jax.numpy as jnp
from jax import lax
from jax.experimental import pallas as pl
from jax.experimental.pallas import tpu as pltpu
from jax.sharding import PartitionSpec as P

DH = 128
DR = 64
DC = 512
PLEN = 512
CLEN = 256
KEYS = PLEN + CLEN
WIDE = 640
PAIRS = 8
NT = (((1,), (1,)), ((), ()))
SCALE = 1.0 / (DH + DR) ** 0.5
F32 = jnp.float32
BF16 = jnp.bfloat16
MESH = pl.DeviceIdType.MESH


def remote(src, dst, send, recv, device):
    return pltpu.make_async_remote_copy(
        src_ref=src, dst_ref=dst, send_sem=send, recv_sem=recv, device_id=device, device_id_type=MESH
    )


def kernel(
    len_ref, plat_ref, prope_ref, clat_ref, crope_ref, q_ref, qr_ref, g_ref, wk_ref, wv_ref,
    glat_ref, grope_ref, gwk_ref, gwv_ref,
    gz, lat, lat_t, rsel, dkv, lacc, racc,
    wpart, crecv, csum, a1recv, a1sum, a2recv, b1recv, b1sum, b2recv,
    lpart, l1recv, l2src, l2recv, l3src, l3recv,
    gz_send, gz_recv, gx_send, gx_recv, gy_send, gy_recv,
    c_send, c_recv, a1_send, a1_recv, a2_send, a2_recv, b1_send, b1_recv, b2_send, b2_recv,
    l1_send, l1_recv, l2_send, l2_recv, l3_send, l3_recv,
):
    step = pl.program_id(0)
    dp, sample, z = lax.axis_index("dp"), lax.axis_index("sample"), lax.axis_index("head")
    x_lo, core = dp // 2, dp % 2
    y, x_hi = sample // 2, sample % 2
    x = x_hi * 2 + x_lo

    def at_core():
        return {"dp": x_lo * 2 + 1 - core}

    def at_x(d):
        to = (x + d) % 4
        return {"dp": (to % 2) * 2 + core, "sample": y * 2 + to // 2}

    def at_y(d):
        return {"sample": ((y + d) % 4) * 2 + x_hi}

    def at_z(d):
        return {"head": (z + d) % 8}

    def gather_z(d):
        return remote(gz.at[z], gz.at[z], gz_send.at[d - 1], gz_recv.at[d - 1], at_z(d))

    def gather_x():
        return remote(lat.at[sample], lat.at[sample], gx_send, gx_recv, at_x(2))

    def gather_y(d):
        mine = pl.ds(y * 2, 2)
        return remote(lat.at[mine], lat.at[mine], gy_send.at[d - 1], gy_recv.at[d - 1], at_y(d))

    def swap_core(i, lo):
        return remote(wpart.at[i, lo, 1 - core], crecv.at[i, lo], c_send.at[i, lo], c_recv.at[i, lo], at_core())

    def a_first(i, d):
        to = (x + d) % 4
        return remote(csum.at[i, 0, to % 2, :, to // 2], a1recv.at[i, d - 1], a1_send.at[i, d - 1], a1_recv.at[i, d - 1], at_x(d))

    def a_second(i, d):
        return remote(a1sum.at[i, (y + d) % 4], a2recv.at[i, d - 1], a2_send.at[i, d - 1], a2_recv.at[i, d - 1], at_y(d))

    def b_first(i, d):
        return remote(csum.at[i, 1, :, (y + d) % 4], b1recv.at[i, d - 1], b1_send.at[i, d - 1], b1_recv.at[i, d - 1], at_y(d))

    def b_second(i, d):
        to = (x + d) % 4
        return remote(b1sum.at[i, to % 2, to // 2], b2recv.at[i, d - 1], b2_send.at[i, d - 1], b2_recv.at[i, d - 1], at_x(d))

    def l_first(d):
        return remote(lpart.at[(y + d) % 4], l1recv.at[d - 1], l1_send.at[d - 1], l1_recv.at[d - 1], at_y(d))

    def l_second(d):
        return remote(l2src.at[(z + d) % 8], l2recv.at[d - 1], l2_send.at[d - 1], l2_recv.at[d - 1], at_z(d))

    def l_third():
        return remote(l3src.at[1 - x_hi], l3recv, l3_send, l3_recv, at_x(2))

    @pl.when(step == 0)
    def _():
        barrier = pltpu.get_barrier_semaphore()
        peers = [at_core()] + [at_x(d) for d in (1, 2, 3)] + [at_y(d) for d in (1, 2, 3)] + [at_z(d) for d in range(1, 8)]
        for peer in peers:
            pl.semaphore_signal(barrier, inc=1, device_id=peer, device_id_type=MESH)
        wide = jnp.concatenate(
            [plat_ref[...].astype(F32), prope_ref[...].astype(F32), jnp.zeros((8, 768 - DC - DR), F32)], 1
        )
        gz[z] = jnp.concatenate([wide[:, :384], wide[:, 384:]], 0).astype(BF16)
        pl.semaphore_wait(barrier, len(peers))
        for d in range(1, 8):
            gather_z(d).start()
        lat[pl.ds(8, 4), :, :DC] = clat_ref[...].reshape(4, 64, DC)
        lat[pl.ds(8, 4), :, DC:] = jnp.concatenate(
            [crope_ref[...], jnp.zeros((CLEN, WIDE - DC - DR), BF16)], 1
        ).reshape(4, 64, WIDE - DC)
        lacc[...] = jnp.zeros_like(lacc)
        racc[...] = jnp.zeros_like(racc)
        for d in range(1, 8):
            gather_z(d).wait()
        block = gz[...].astype(F32)
        lat[sample] = jnp.concatenate([block[:, :8], block[:, 8:, : WIDE - 384]], 2).reshape(64, WIDE).astype(BF16)
        gather_x().start()
        gather_x().wait()
        for d in (1, 2, 3):
            gather_y(d).start()
        for d in (1, 2, 3):
            gather_y(d).wait()
        rows = lat[...].reshape(KEYS, WIDE)
        lat_t[...] = rows[:, :DC].T
        rsel[0] = rows[:, DC:]
        rsel[1] = jnp.concatenate([jnp.zeros((KEYS, DR), BF16), rows[:, DC : DC + DR]], 1)

    @pl.when((step >= 1) & (step < PAIRS + 1))
    def _():
        i = step - 1
        for lo in range(2):
            swap_core(i, lo).wait()
        for half in range(2):
            for lo in range(2):
                csum[i, half, lo] = (
                    wpart[i, lo, core, half].astype(F32) + crecv[i, lo, half].astype(F32)
                ).astype(BF16)
        for d in (1, 2, 3):
            a_first(i, d).start()
            b_first(i, d).start()

    @pl.when((step >= 2) & (step < PAIRS + 2))
    def _():
        i = step - 2
        for d in (1, 2, 3):
            a_first(i, d).wait()
            b_first(i, d).wait()
        a = csum[i, 0, x_lo, :, x_hi].astype(F32)
        b = csum[i, 1, :, y].astype(F32)
        for d in range(3):
            a = a + a1recv[i, d].astype(F32)
            b = b + b1recv[i, d].astype(F32)
        a1sum[i] = a.astype(BF16)
        b1sum[i] = b.astype(BF16)
        for d in (1, 2, 3):
            a_second(i, d).start()
            b_second(i, d).start()

    @pl.when(step >= 3)
    def _():
        i = step - 3
        for d in (1, 2, 3):
            a_second(i, d).wait()
            b_second(i, d).wait()
        a = a1sum[i, y].astype(F32)
        b = b1sum[i, x_lo, x_hi].astype(F32)
        for d in range(3):
            a = a + a2recv[i, d].astype(F32)
            b = b + b2recv[i, d].astype(F32)
        cols = pl.ds(pl.multiple_of(i * 256, 256), 256)
        gwk_ref[:, cols] = a
        gwv_ref[:, cols] = b

    @pl.when(step == PAIRS)
    def _():
        for d in (1, 2, 3):
            l_first(d).wait()
        total = lpart[y].astype(F32)
        for d in range(3):
            total = total + l1recv[d].astype(F32)
        total = total.reshape(2, 8, 8, WIDE)
        l2src[...] = jnp.concatenate([total[0], total[1]], 1).astype(BF16)
        for d in range(1, 8):
            l_second(d).start()

    @pl.when(step == PAIRS + 1)
    def _():
        for d in range(1, 8):
            l_second(d).wait()
        total = l2src[z].astype(F32)
        for d in range(7):
            total = total + l2recv[d].astype(F32)
        l3src[...] = total.reshape(2, 8, WIDE)
        l_third().start()

    @pl.when(step == PAIRS + 2)
    def _():
        l_third().wait()
        total = l3src[x_hi] + l3recv[...]
        glat_ref[...] = total[:, :DC]
        grope_ref[...] = total[:, DC : DC + DR]

    @pl.when(step < PAIRS)
    def _():
        live = lax.broadcasted_iota(jnp.int32, (CLEN, 256), 0) < len_ref[0, 0]
        g = jnp.where(live, g_ref[...], jnp.zeros((), BF16))
        rows = lat[:, :, :DC].reshape(KEYS, DC)
        keys = jnp.dot(rows, wk_ref[...], preferred_element_type=F32).astype(BF16)
        vals = jnp.dot(rows, wv_ref[...], preferred_element_type=F32).astype(BF16)
        qr = qr_ref[...]
        see = lax.broadcasted_iota(jnp.int32, (CLEN, CLEN), 0) <= lax.broadcasted_iota(jnp.int32, (CLEN, CLEN), 1)
        for h in range(2):
            cols = slice(h * DH, (h + 1) * DH)
            kx = jnp.concatenate([keys[:, cols], rsel[h]], 1)
            qx = jnp.concatenate([q_ref[:, cols], qr], 1)
            gh = g[:, cols]
            s = lax.dot_general(kx, qx, NT, preferred_element_type=F32)
            s = jnp.concatenate([s[:PLEN], jnp.where(see, s[PLEN:], -1e30)], 0)
            m = jnp.max(s, axis=0, keepdims=True)
            p = jnp.exp2((s - m) * (SCALE * math.log2(math.e)))
            p = p * (1.0 / jnp.sum(p, axis=0, keepdims=True))
            pb = p.astype(BF16)
            dprob = lax.dot_general(vals[:, cols], gh, NT, preferred_element_type=F32)
            delta = jnp.sum(pb.astype(F32) * dprob, axis=0, keepdims=True)
            ds = (p * (dprob - delta)).astype(BF16)
            dk = jnp.dot(ds, qx, preferred_element_type=F32)
            dkv[0, :, cols] = (dk[:, :DH] * SCALE).astype(BF16)
            racc[h] += dk[:PLEN, DH:]
            dkv[1, :, cols] = jnp.dot(pb, gh, preferred_element_type=F32).astype(BF16)
        for half in range(2):
            part = jnp.dot(lat_t[...], dkv[half], preferred_element_type=F32).astype(BF16)
            part = part.reshape(2, 2, 4, 2, 16, 256)
            wpart[step, :, :, half] = part
        for lo in range(2):
            swap_core(step, lo).start()
        lacc[...] += lax.dot_general(dkv[0, :PLEN], wk_ref[...], NT, preferred_element_type=F32)
        lacc[...] += lax.dot_general(dkv[1, :PLEN], wv_ref[...], NT, preferred_element_type=F32)

    @pl.when(step == PAIRS - 1)
    def _():
        lpart[:, :, :DC] = lacc[...].astype(BF16).reshape(4, 128, DC)
        rope = (racc[0, :, :DR] + racc[1, :, DR:]) * SCALE
        rope = jnp.concatenate([rope, jnp.zeros((PLEN, WIDE - DC - DR), F32)], 1)
        lpart[:, :, DC:] = rope.astype(BF16).reshape(4, 128, WIDE - DC)
        for d in (1, 2, 3):
            l_first(d).start()

    @pl.when(step == PAIRS + 2)
    def _():
        pass


def local(prompt_latent, prompt_rope, comp_latent, comp_rope, query_nope, query_rope, grad_out, lengths, w_uk, w_uv):
    def whole(*shape):
        return pl.BlockSpec(shape, lambda i: (0,) * len(shape))

    def part(rows, cols):
        return pl.BlockSpec((rows, cols), lambda i: (0, jnp.minimum(i, PAIRS - 1)))

    dma = pltpu.SemaphoreType.DMA
    outs = pl.pallas_call(
        kernel,
        grid=(PAIRS + 3,),
        in_specs=[
            pl.BlockSpec(memory_space=pltpu.SMEM),
            whole(8, DC), whole(8, DR), whole(CLEN, DC), whole(CLEN, DR),
            part(CLEN, 256), part(CLEN, 128), part(CLEN, 256), part(DC, 256), part(DC, 256),
        ],
        out_specs=[whole(8, DC), whole(8, DR), whole(16, 2048), whole(16, 2048)],
        out_shape=[
            jax.ShapeDtypeStruct((8, DC), F32), jax.ShapeDtypeStruct((8, DR), F32),
            jax.ShapeDtypeStruct((16, 2048), F32), jax.ShapeDtypeStruct((16, 2048), F32),
        ],
        scratch_shapes=[
            pltpu.VMEM((8, 16, 384), BF16), pltpu.VMEM((12, 64, WIDE), BF16), pltpu.VMEM((DC, KEYS), BF16),
            pltpu.VMEM((2, KEYS, DH), BF16), pltpu.VMEM((2, KEYS, 256), BF16),
            pltpu.VMEM((PLEN, DC), F32), pltpu.VMEM((2, PLEN, 128), F32),
            pltpu.VMEM((PAIRS, 2, 2, 2, 4, 2, 16, 256), BF16),
            pltpu.VMEM((PAIRS, 2, 2, 4, 2, 16, 256), BF16),
            pltpu.VMEM((PAIRS, 2, 2, 4, 2, 16, 256), BF16),
            pltpu.VMEM((PAIRS, 3, 4, 16, 256), BF16), pltpu.VMEM((PAIRS, 4, 16, 256), BF16),
            pltpu.VMEM((PAIRS, 3, 16, 256), BF16),
            pltpu.VMEM((PAIRS, 3, 2, 2, 16, 256), BF16), pltpu.VMEM((PAIRS, 2, 2, 16, 256), BF16),
            pltpu.VMEM((PAIRS, 3, 16, 256), BF16),
            pltpu.VMEM((4, 128, WIDE), BF16), pltpu.VMEM((3, 128, WIDE), BF16),
            pltpu.VMEM((8, 16, WIDE), BF16), pltpu.VMEM((7, 16, WIDE), BF16),
            pltpu.VMEM((2, 8, WIDE), F32), pltpu.VMEM((8, WIDE), F32),
            dma((7,)), dma((7,)), dma, dma, dma((3,)), dma((3,)),
            dma((PAIRS, 2)), dma((PAIRS, 2)),
            dma((PAIRS, 3)), dma((PAIRS, 3)), dma((PAIRS, 3)), dma((PAIRS, 3)),
            dma((PAIRS, 3)), dma((PAIRS, 3)), dma((PAIRS, 3)), dma((PAIRS, 3)),
            dma((3,)), dma((3,)), dma((7,)), dma((7,)), dma, dma,
        ],
        compiler_params=pltpu.CompilerParams(
            vmem_limit_bytes=56 * 1024 * 1024, collective_id=0, has_side_effects=True
        ),
        cost_estimate=pl.CostEstimate(flops=13_000_000_000, bytes_accessed=8_000_000, transcendentals=3_200_000),
        name="mla_backward",
    )(
        lengths, prompt_latent[0], prompt_rope[0], comp_latent[0, 0], comp_rope[0, 0],
        query_nope[0, 0], query_rope[0, 0], grad_out[0, 0], w_uk, w_uv,
    )
    return (outs[0][None], outs[1][None], outs[2], outs[3])


def solution(mesh):
    in_specs = (
        P("dp", ("sample", "head"), None),
        P("dp", ("sample", "head"), None),
        P("dp", "sample", None, None),
        P("dp", "sample", None, None),
        P("dp", "sample", None, "head"),
        P("dp", "sample", None, "head"),
        P("dp", "sample", None, "head"),
        P("dp", "sample"),
        P(None, "head"),
        P(None, "head"),
    )
    out_specs = (
        P("dp", ("sample", "head"), None),
        P("dp", ("sample", "head"), None),
        P(("dp", "sample"), "head"),
        P(("dp", "sample"), "head"),
    )
    return jax.shard_map(local, mesh=mesh, in_specs=in_specs, out_specs=out_specs, check_vma=False)
```

time: 1100 us -> 95.2 us (0.09)
  waiting for transfers between devices: 610 us -> 0 us
  blocking collectives: 361 us -> 0 us
  Pallas kernels: 0 us -> 86.4 us
  matrix products: 70.2 us -> 0 us
  local copies, waits for them, and re-layouts: 26.3 us -> 7.23 us
  between operations: 17.1 us -> 1.29 us
  other arithmetic: 14.2 us -> 0 us
    unnamed x5 -> x0, waiting for transfers between devices: 610 us -> none
    all_gather x2 -> x0, blocking collectives: 361 us -> none  [the longest x1 187 us: local(): lax.all_gather(prompt_latent, ('sample', 'head'), axis=1, tiled=True)]
    pallas_call x0 -> x1, Pallas kernels: none -> 86.4 us  [local(): pl.pallas_call(kernel, grid=(PAIRS + 3,), in_specs=[pl.BlockSpec(memory_s...]
    dot_general x14 -> x0, matrix products: 56.6 us -> none  [the longest x1 8.25 us: attend(): jnp.einsum('rhd,khd->hrk', query_nope, all_keys, preferred_element_type=j...]
    sub x1 -> x0, matrix products: 13.6 us -> none  [attend(): probs = jax.nn.softmax(score, axis=-1)]
  transfers between devices with their start and end apart: 3 -> 0, of which waited for: 1 -> 0; matrix products, arithmetic and copies ran while one was open for 3% -> 0% of each run, Pallas kernels for 0% -> 0%
where the time goes in v1:
time: 95.2 us; the launch traced here: 94.9 us
  Pallas kernels  86.4 us (91%)
  local copies, waits for them, and re-layouts  7.23 us (8%)
  between operations  1.29 us (1%)
    pallas_call x1, Pallas kernels, local(): pl.pallas_call(kernel, grid=(PAIRS + 3,), in_specs=[pl.BlockSpec(memory_s...  86.4 us
    unnamed x5, local copies, waits for them, and re-layouts  7.23 us

profile of v1, /device:TPU:2, one launch (start us, length us, event | category | flops | bytes accessed | tf_op | source)
XLA Modules:
  0.0 94.9 jit_solution(4803035403022048348)
XLA Ops:
  1.3 1.5 %copy.14 = bf16[1,1,256,64]{3,2,1,0:T(8,128)(2,1)} copy(bf16[1,1,256,64]{2,3,1,0:T(8,128)(2,1)} %param.13) | data formatting | bytes 65536 | tf_op args[3]
  2.8 86.4 %mla_backward.1 = (f32[8,512]{1,0:T(8,128)}, f32[8,64]{1,0:T(8,128)}, f32[16,2048]{1,0:T(8,128)}, f32[16,2048]{1,0:T(8,128)}) custom-call(s32[1,1]{1,0:T(1,128)S(6)} %copy.19.len_ref, bf16[8,512]{1,0:T(8,128)(2,1)} %bitcast.16, bf16[8,64]{1,0:T(8,128)(2,1)} %bitcast.17, bf16[256,512]{1,0:T(8,128)(2,1)} %bitcast.15, bf16[256,64]{1,0:T(8,128)(2,1)} %bitcast.9, ...), custom_call_target="tpu_custom_call" | custom-call | flops 12999999488 | bytes 8000000 | tf_op jit(solution)/shard_map/mla_backward/pallas_call | solution.py:263
  89.2 1.3 %copy.20 = f32[1,8,512]{2,1,0:T(8,128)} copy(f32[1,8,512]{2,1,0:T(8,128)} %bitcast.10) | data formatting | bytes 32768
  90.5 1.3 %copy.21 = f32[1,8,64]{2,1,0:T(8,128)} copy(f32[1,8,64]{2,1,0:T(8,128)} %bitcast.11) | data formatting | bytes 4096
  91.8 1.6 %copy.22 = f32[16,2048]{1,0:T(8,128)} copy(f32[16,2048]{1,0:T(8,128)} %get-tuple-element.18) | data formatting | bytes 262144
  93.4 1.6 %copy.23 = f32[16,2048]{1,0:T(8,128)} copy(f32[16,2048]{1,0:T(8,128)} %get-tuple-element.19) | data formatting | bytes 262144

commit v2 on v0

v2 whole, which is shorter than its diff:
```python
import math

import jax
import jax.numpy as jnp
from jax import lax
from jax.experimental import pallas as pl
from jax.experimental.pallas import tpu as pltpu
from jax.sharding import PartitionSpec as P

DH = 128
DR = 64
DC = 512
PLEN = 512
CLEN = 256
KEYS = PLEN + CLEN
WIDE = 640
PACK = 384
PAIRS = 8
NT = (((1,), (1,)), ((), ()))
SCALE = 1.0 / (DH + DR) ** 0.5
F32 = jnp.float32
BF16 = jnp.bfloat16
MESH = pl.DeviceIdType.MESH
OVER_XY = ((0, 0), (2, 0), (0, 1), (0, 3), (2, 1), (2, 3), (0, 2), (2, 2))
OVER_Z = (0, 1, 7, 2, 6, 3, 5, 4)
ALL_XY = tuple((dx, dy) for dx in range(4) for dy in range(4) if dx or dy)


def kernel(
    len_ref, plat_hbm, prope_hbm, clat_hbm, crope_hbm, q_hbm, qr_hbm, g_hbm, wk_hbm, wv_hbm,
    glat_ref, gw_ref,
    plat, prope, clat, crope, q_ref, qr_ref, g_ref, wk_ref, wv_ref,
    gz, lat, lat_t, rsel, kv, dkv, lacc, racc,
    wpart, crecv, csum, drecv, lpart, l1recv, l2src, l2own, l2recv,
    load, gz_send, gz_recv, gy_send, gy_recv, c_send, c_recv, d_send, d_recv, l1_send, l1_recv, l2_send, l2_recv,
):
    step = pl.program_id(0)
    dp, sample, z = lax.axis_index("dp"), lax.axis_index("sample"), lax.axis_index("head")
    x_lo, core = dp // 2, dp % 2
    y, x_hi = sample // 2, sample % 2
    x = x_hi * 2 + x_lo

    def at_xy(dx, dy):
        to = (x + dx) % 4
        return {"dp": (to % 2) * 2 + core, "sample": ((y + dy) % 4) * 2 + to // 2}

    def at_z(d):
        return {"head": (z + d) % 8}

    other_core = {"dp": x_lo * 2 + 1 - core}

    def remote(src, dst, send, recv, device):
        return pltpu.make_async_remote_copy(
            src_ref=src, dst_ref=dst, send_sem=send, recv_sem=recv, device_id=device, device_id_type=MESH
        )

    def arrived(ref, sem):
        pltpu.make_async_copy(ref, ref, sem).wait()

    def swap_core(i):
        return remote(wpart.at[i, :, 1 - core], crecv.at[i], c_send.at[i], c_recv.at[i], other_core)

    def project(first, count):
        rows = lat[first : first + count, :, :DC].reshape(count * 64, DC)

        def pair(i, carry):
            cols = pl.ds(pl.multiple_of(i * 256, 256), 256)
            for half, w in enumerate((wk_ref, wv_ref)):
                kv[i, half, first * 64 : (first + count) * 64] = jnp.dot(
                    rows, w[:, cols], preferred_element_type=F32
                ).astype(BF16)
            return carry

        lax.fori_loop(0, PAIRS, pair, 0)
        tokens = slice(first * 64, (first + count) * 64)
        lat_t[:, tokens] = rows.T
        rope = lat[first : first + count, :, DC:].reshape(count * 64, DH)
        rsel[0, tokens] = rope
        rsel[1, tokens] = jnp.concatenate([jnp.zeros((count * 64, DR), BF16), rope[:, :DR]], 1)

    @pl.when(step == 0)
    def _():
        pairs = (
            (plat_hbm, plat), (prope_hbm, prope), (clat_hbm, clat), (crope_hbm, crope), (wk_hbm, wk_ref),
            (wv_hbm, wv_ref), (q_hbm, q_ref), (qr_hbm, qr_ref), (g_hbm, g_ref),
        )
        loads = [pltpu.make_async_copy(src, dst, load.at[n]) for n, (src, dst) in enumerate(pairs)]
        for copy in loads:
            copy.start()
        barrier = pltpu.get_barrier_semaphore()
        peers = [other_core] + [at_xy(dx, dy) for dx, dy in ALL_XY] + [at_z(d) for d in range(1, 8)]
        for peer in peers:
            pl.semaphore_signal(barrier, inc=1, device_id=peer, device_id_type=MESH)
        loads[0].wait()
        loads[1].wait()
        wide = jnp.concatenate([plat[...].astype(F32), prope[...].astype(F32), jnp.zeros((8, 2 * PACK - DC - DR), F32)], 1)
        gz[0] = jnp.concatenate([wide[:, :PACK], wide[:, PACK:]], 0).astype(BF16)
        pl.semaphore_wait(barrier, len(peers))
        for k in range(1, 8):
            remote(gz.at[0], gz.at[k], gz_send, gz_recv, at_z(8 - OVER_Z[k])).start()
        loads[2].wait()
        loads[3].wait()
        lat[8:12, :, :DC] = clat[...].reshape(4, 64, DC)
        rope = jnp.concatenate([crope[...].astype(F32).T, jnp.zeros((CLEN, WIDE - DC - DR), F32)], 1)
        lat[8:12, :, DC:] = rope.astype(BF16).reshape(4, 64, WIDE - DC)
        lacc[...] = jnp.zeros_like(lacc)
        racc[...] = jnp.zeros_like(racc)
        loads[4].wait()
        loads[5].wait()
        project(8, 4)
        arrived(gz.at[pl.ds(1, 7)], gz_recv)
        block = gz[...].astype(F32)
        lat[0] = jnp.concatenate([block[:, :8], block[:, 8:, : WIDE - PACK]], 2).reshape(64, WIDE).astype(BF16)
        for b in range(1, 8):
            dx, dy = OVER_XY[b]
            remote(lat.at[0], lat.at[b], gy_send, gy_recv.at[b // 4], at_xy(4 - dx, 4 - dy)).start()
        for copy in loads[6:]:
            copy.wait()
        live = lax.broadcasted_iota(jnp.int32, g_ref.shape, 0) < len_ref[0, 0]
        g_ref[...] = jnp.where(live, g_ref[...], jnp.zeros((), BF16))
        arrived(lat.at[pl.ds(1, 3)], gy_recv.at[0])
        project(0, 4)
        arrived(lat.at[pl.ds(4, 4)], gy_recv.at[1])
        project(4, 4)
        arrived(gz.at[pl.ds(1, 7)], gz_send)
        arrived(lat.at[pl.ds(1, 7)], gy_send)

    @pl.when(step < PAIRS)
    def _():
        pair = pl.ds(pl.multiple_of(step * 256, 256), 256)
        qr = qr_ref[:, pl.ds(pl.multiple_of(step * DH, DH), DH)]
        see = lax.broadcasted_iota(jnp.int32, (CLEN, CLEN), 0) <= lax.broadcasted_iota(jnp.int32, (CLEN, CLEN), 1)
        keys, vals = kv[step, 0], kv[step, 1]
        q, g = q_ref[:, pair], g_ref[:, pair]
        for h in range(2):
            cols = slice(h * DH, (h + 1) * DH)
            kx = jnp.concatenate([keys[:, cols], rsel[h]], 1)
            qx = jnp.concatenate([q[:, cols], qr], 1)
            gh = g[:, cols]
            s = lax.dot_general(kx, qx, NT, preferred_element_type=F32)
            s = jnp.concatenate([s[:PLEN], jnp.where(see, s[PLEN:], -1e30)], 0)
            m = jnp.max(s, axis=0, keepdims=True)
            p = jnp.exp2((s - m) * (SCALE * math.log2(math.e)))
            p = p * (1.0 / jnp.sum(p, axis=0, keepdims=True))
            pb = p.astype(BF16)
            dprob = lax.dot_general(vals[:, cols], gh, NT, preferred_element_type=F32)
            delta = jnp.sum(pb.astype(F32) * dprob, axis=0, keepdims=True)
            ds = (p * (dprob - delta)).astype(BF16)
            dk = jnp.dot(ds, qx, preferred_element_type=F32)
            dkv[:, cols] = (dk[:, :DH] * SCALE).astype(BF16)
            racc[h] += dk[:PLEN, DH:]
            dkv[:, 256 + h * DH : 256 + (h + 1) * DH] = jnp.dot(pb, gh, preferred_element_type=F32).astype(BF16)
        both = jnp.concatenate([wk_ref[:, pair], wv_ref[:, pair]], 1)
        lacc[...] += lax.dot_general(dkv[:PLEN], both, NT, preferred_element_type=F32)

    @pl.when(step == PAIRS - 1)
    def _():
        lpart[:, :, :DC] = lacc[...].astype(BF16).reshape(8, 64, DC)
        rope = (racc[0, :, :DR] + racc[1, :, DR:]) * SCALE
        rope = jnp.concatenate([rope, jnp.zeros((PLEN, WIDE - DC - DR), F32)], 1)
        lpart[:, :, DC:] = rope.astype(BF16).reshape(8, 64, WIDE - DC)
        for b in range(1, 8):
            remote(lpart.at[b], l1recv.at[b - 1], l1_send, l1_recv, at_xy(*OVER_XY[b])).start()

    @pl.when((step >= 1) & (step < PAIRS + 1))
    def _():
        i = step - 1
        swap_core(i).wait()
        for lo in range(2):
            csum[i, lo] = (wpart[i, lo, core].astype(F32) + crecv[i, lo].astype(F32)).astype(BF16)
        for n, (dx, dy) in enumerate(ALL_XY):
            to = (x + dx) % 4
            remote(
                csum.at[i, to % 2, (y + dy) % 4, to // 2], drecv.at[i, n], d_send.at[i], d_recv.at[i], at_xy(dx, dy)
            ).start()

    @pl.when(step < PAIRS)
    def _():
        part = jnp.dot(lat_t[...], dkv[...], preferred_element_type=F32).astype(BF16)
        wpart[step] = part.reshape(2, 2, 4, 2, 16, 512)
        swap_core(step).start()

    @pl.when(step >= 2)
    def _():
        i = step - 2
        arrived(drecv.at[i], d_recv.at[i])
        total = csum[i, x_lo, y, x_hi].astype(F32)
        for n in range(15):
            total = total + drecv[i, n].astype(F32)
        cols = pl.ds(pl.multiple_of(i * 256, 256), 256)
        gw_ref[0, :, cols] = total[:, :256]
        gw_ref[1, :, cols] = total[:, 256:]
        arrived(drecv.at[i], d_send.at[i])

    @pl.when(step == PAIRS)
    def _():
        arrived(l1recv, l1_recv)
        total = lpart[0].astype(F32)
        for b in range(7):
            total = total + l1recv[b].astype(F32)
        total = jnp.concatenate([total, jnp.zeros((64, 2 * PACK - WIDE), F32)], 1).reshape(8, 8, 2 * PACK)
        total = jnp.concatenate([total[:, :, :PACK], total[:, :, PACK:]], 1)
        l2own[...] = total[0]
        l2src[...] = total.astype(BF16)
        for k in range(1, 8):
            remote(l2src.at[k], l2recv.at[k - 1], l2_send, l2_recv, at_z(OVER_Z[k])).start()

    @pl.when(step == PAIRS + 1)
    def _():
        arrived(l2recv, l2_recv)
        total = l2own[...]
        for k in range(7):
            total = total + l2recv[k].astype(F32)
        glat_ref[...] = jnp.concatenate([total[:8], total[8:, : WIDE - PACK]], 1)
        arrived(l1recv, l1_send)
        arrived(l2recv, l2_send)


def finish(lat_ref, w_ref, glat_ref, grope_ref, gwk_ref, gwv_ref):
    glat_ref[...] = lat_ref[:, :DC]
    grope_ref[...] = lat_ref[:, DC : DC + DR]
    gwk_ref[...] = w_ref[0]
    gwv_ref[...] = w_ref[1]


def local(prompt_latent, prompt_rope, comp_latent, comp_rope, query_nope, query_rope, grad_out, lengths, w_uk, w_uv):
    def whole(*shape):
        return pl.BlockSpec(shape, lambda i: (0,) * len(shape))

    vmem, dma = pltpu.VMEM, pltpu.SemaphoreType.DMA
    lat, weights = pl.pallas_call(
        kernel,
        grid=(PAIRS + 2,),
        in_specs=[pl.BlockSpec(memory_space=pltpu.SMEM)] + [pl.BlockSpec(memory_space=pl.ANY)] * 9,
        out_specs=[whole(8, WIDE), whole(2, 16, 2048)],
        out_shape=[jax.ShapeDtypeStruct((8, WIDE), F32), jax.ShapeDtypeStruct((2, 16, 2048), F32)],
        scratch_shapes=[
            vmem((8, DC), BF16), vmem((8, DR), BF16), vmem((CLEN, DC), BF16), vmem((DR, CLEN), BF16),
            vmem((CLEN, 2048), BF16), vmem((CLEN, 1024), BF16), vmem((CLEN, 2048), BF16),
            vmem((DC, 2048), BF16), vmem((DC, 2048), BF16),
            vmem((8, 16, PACK), BF16), vmem((12, 64, WIDE), BF16), vmem((DC, KEYS), BF16), vmem((2, KEYS, DH), BF16),
            vmem((PAIRS, 2, KEYS, 256), BF16), vmem((KEYS, 512), BF16), vmem((PLEN, DC), F32), vmem((2, PLEN, DH), F32),
            vmem((PAIRS, 2, 2, 4, 2, 16, 512), BF16),
            vmem((PAIRS, 2, 4, 2, 16, 512), BF16), vmem((PAIRS, 2, 4, 2, 16, 512), BF16),
            vmem((PAIRS, 15, 16, 512), BF16),
            vmem((8, 64, WIDE), BF16), vmem((7, 64, WIDE), BF16),
            vmem((8, 16, PACK), BF16), vmem((16, PACK), F32), vmem((7, 16, PACK), BF16),
            dma((9,)), dma, dma, dma, dma((2,)), dma((PAIRS,)), dma((PAIRS,)), dma((PAIRS,)), dma((PAIRS,)),
            dma, dma, dma, dma,
        ],
        compiler_params=pltpu.CompilerParams(
            vmem_limit_bytes=56 * 1024 * 1024, collective_id=0, has_side_effects=True
        ),
        cost_estimate=pl.CostEstimate(flops=13_000_000_000, bytes_accessed=8_000_000, transcendentals=3_200_000),
        name="mla_backward",
    )(
        lengths, prompt_latent[0], prompt_rope[0], comp_latent[0, 0], comp_rope[0, 0].T,
        query_nope[0, 0], query_rope[0, 0], grad_out[0, 0], w_uk, w_uv,
    )
    outs = pl.pallas_call(
        finish,
        out_shape=[
            jax.ShapeDtypeStruct((8, DC), F32), jax.ShapeDtypeStruct((8, DR), F32),
            jax.ShapeDtypeStruct((16, 2048), F32), jax.ShapeDtypeStruct((16, 2048), F32),
        ],
        name="outputs",
    )(lat, weights)
    return (outs[0][None], outs[1][None], outs[2], outs[3])


def solution(mesh):
    in_specs = (
        P("dp", ("sample", "head"), None),
        P("dp", ("sample", "head"), None),
        P("dp", "sample", None, None),
        P("dp", "sample", None, None),
        P("dp", "sample", None, "head"),
        P("dp", "sample", None, "head"),
        P("dp", "sample", None, "head"),
        P("dp", "sample"),
        P(None, "head"),
        P(None, "head"),
    )
    out_specs = (
        P("dp", ("sample", "head"), None),
        P("dp", ("sample", "head"), None),
        P(("dp", "sample"), "head"),
        P(("dp", "sample"), "head"),
    )
    return jax.shard_map(local, mesh=mesh, in_specs=in_specs, out_specs=out_specs, check_vma=False)
```

time: 1100 us -> 79.6 us (0.07)
  waiting for transfers between devices: 610 us -> 0 us
  blocking collectives: 361 us -> 0 us
  Pallas kernels: 0 us -> 76.9 us
  matrix products: 70.2 us -> 0 us
  local copies, waits for them, and re-layouts: 26.3 us -> 0 us
  between operations: 17.1 us -> 1.29 us
  other arithmetic: 14.2 us -> 0 us
    unnamed x5 -> x0, waiting for transfers between devices: 610 us -> none
    all_gather x2 -> x0, blocking collectives: 361 us -> none  [the longest x1 187 us: local(): lax.all_gather(prompt_latent, ('sample', 'head'), axis=1, tiled=True)]
    pallas_call x0 -> x2, Pallas kernels: none -> 76.9 us  [the longest x1 75.2 us: local(): pl.pallas_call(kernel, grid=(PAIRS + 2,), in_specs=[pl.BlockSpec(memory_s...]
    dot_general x14 -> x0, matrix products: 56.6 us -> none  [the longest x1 8.25 us: attend(): jnp.einsum('rhd,khd->hrk', query_nope, all_keys, preferred_element_type=j...]
    unnamed x41 -> x0, local copies, waits for them, and re-layouts: 16.5 us -> none
    sub x1 -> x0, matrix products: 13.6 us -> none  [attend(): probs = jax.nn.softmax(score, axis=-1)]
  transfers between devices with their start and end apart: 3 -> 0, of which waited for: 1 -> 0; matrix products, arithmetic and copies ran while one was open for 3% -> 0% of each run, Pallas kernels for 0% -> 0%
where the time goes in v2:
time: 79.6 us; the launch traced here: 78.2 us
  Pallas kernels  76.9 us (97%)
  between operations  1.29 us (2%)
    pallas_call x1, Pallas kernels, local(): pl.pallas_call(kernel, grid=(PAIRS + 2,), in_specs=[pl.BlockSpec(memory_s...  75.2 us
    pallas_call x1, Pallas kernels, local(): pl.pallas_call(finish, out_shape=[jax.ShapeDtypeStruct((8, DC), F32), jax...  1.68 us

profile of v2, /device:TPU:2, one launch (start us, length us, event | category | flops | bytes accessed | tf_op | source)
XLA Modules:
  0.0 78.2 jit_solution(16790902936349978580)
XLA Ops:
  1.3 75.2 %mla_backward.1 = (f32[8,640]{1,0:T(8,128)}, f32[2,16,2048]{2,1,0:T(8,128)}) custom-call(s32[1,1]{1,0:T(1,128)S(6)} %copy.14.len_ref, bf16[8,512]{1,0:T(8,128)(2,1)} %bitcast.17, bf16[8,64]{1,0:T(8,128)(2,1)} %bitcast.19, bf16[256,512]{1,0:T(8,128)(2,1)} %bitcast.14, bf16[64,256]{1,0:T(8,128)(2,1)} %bitcast.15, bf16[256,2048]{1,0:T(8,128)(2,1)} %bitcast.11, ...), custom_call_target="tpu_custom_call" | custom-call | flops 12999999488 | bytes 8000000 | tf_op jit(solution)/shard_map/mla_backward/pallas_call | solution.py:231
  76.5 1.7 %outputs.1 = (f32[8,512]{1,0:T(8,128)}, f32[8,64]{1,0:T(8,128)}, f32[16,2048]{1,0:T(8,128)}, f32[16,2048]{1,0:T(8,128)}) custom-call(f32[8,640]{1,0:T(8,128)} %get-tuple-element.10.lat_ref, f32[2,16,2048]{2,1,0:T(8,128)} %get-tuple-element.11.w_ref), custom_call_target="tpu_custom_call" | custom-call | tf_op jit(solution)/shard_map/outputs/pallas_call | solution.py:260

commit v3 on v2

--- a/solution.py
+++ b/solution.py
@@ -14,6 +14,8 @@
 CLEN = 256
 KEYS = PLEN + CLEN
 WIDE = 640
+ACOLS = 384
+BCOLS = WIDE - ACOLS
 PACK = 384
 PAIRS = 8
 NT = (((1,), (1,)), ((), ()))
@@ -27,12 +29,13 @@
 
 
 def kernel(
-    len_ref, plat_hbm, prope_hbm, clat_hbm, crope_hbm, q_hbm, qr_hbm, g_hbm, wk_hbm, wv_hbm,
+    len_hbm, plat_hbm, prope_hbm, clat_hbm, crope_hbm, q_hbm, qr_hbm, g_hbm, wk_hbm, wv_hbm,
     glat_ref, gw_ref,
-    plat, prope, clat, crope, q_ref, qr_ref, g_ref, wk_ref, wv_ref,
-    gz, lat, lat_t, rsel, kv, dkv, lacc, racc,
-    wpart, crecv, csum, drecv, lpart, l1recv, l2src, l2own, l2recv,
-    load, gz_send, gz_recv, gy_send, gy_recv, c_send, c_recv, d_send, d_recv, l1_send, l1_recv, l2_send, l2_recv,
+    plat, prope, clat, crope, q_ref, qr_ref, g_ref, wk_ref, wv_ref, len_ref,
+    gz, lat, lat_t, rsel, kv, dkv, dkv_new, lacc, racc,
+    wpart, crecv, csum, drecv, apart, a1recv, a2src, a2recv, bpart, b1recv, b2src, b2recv,
+    load, gz_send, gz_recv, gy_send, gy_recv, c_send, c_recv, d_send, d_recv,
+    a1_send, a1_recv, a2_send, a2_recv, b1_send, b1_recv, b2_send, b2_recv,
 ):
     step = pl.program_id(0)
     dp, sample, z = lax.axis_index("dp"), lax.axis_index("sample"), lax.axis_index("head")
@@ -82,7 +85,7 @@
     def _():
         pairs = (
             (plat_hbm, plat), (prope_hbm, prope), (clat_hbm, clat), (crope_hbm, crope), (wk_hbm, wk_ref),
-            (wv_hbm, wv_ref), (q_hbm, q_ref), (qr_hbm, qr_ref), (g_hbm, g_ref),
+            (wv_hbm, wv_ref), (q_hbm, q_ref), (qr_hbm, qr_ref), (g_hbm, g_ref), (len_hbm, len_ref),
         )
         loads = [pltpu.make_async_copy(src, dst, load.at[n]) for n, (src, dst) in enumerate(pairs)]
         for copy in loads:
@@ -103,6 +106,7 @@
         lat[8:12, :, :DC] = clat[...].reshape(4, 64, DC)
         rope = jnp.concatenate([crope[...].astype(F32).T, jnp.zeros((CLEN, WIDE - DC - DR), F32)], 1)
         lat[8:12, :, DC:] = rope.astype(BF16).reshape(4, 64, WIDE - DC)
+        dkv[...] = jnp.zeros_like(dkv)
         lacc[...] = jnp.zeros_like(lacc)
         racc[...] = jnp.zeros_like(racc)
         loads[4].wait()
@@ -116,7 +120,7 @@
             remote(lat.at[0], lat.at[b], gy_send, gy_recv.at[b // 4], at_xy(4 - dx, 4 - dy)).start()
         for copy in loads[6:]:
             copy.wait()
-        live = lax.broadcasted_iota(jnp.int32, g_ref.shape, 0) < len_ref[0, 0]
+        live = lax.broadcasted_iota(jnp.int32, g_ref.shape, 0) < len_ref[...]
         g_ref[...] = jnp.where(live, g_ref[...], jnp.zeros((), BF16))
         arrived(lat.at[pl.ds(1, 3)], gy_recv.at[0])
         project(0, 4)
@@ -125,46 +129,16 @@
         arrived(gz.at[pl.ds(1, 7)], gz_send)
         arrived(lat.at[pl.ds(1, 7)], gy_send)
 
-    @pl.when(step < PAIRS)
-    def _():
-        pair = pl.ds(pl.multiple_of(step * 256, 256), 256)
-        qr = qr_ref[:, pl.ds(pl.multiple_of(step * DH, DH), DH)]
-        see = lax.broadcasted_iota(jnp.int32, (CLEN, CLEN), 0) <= lax.broadcasted_iota(jnp.int32, (CLEN, CLEN), 1)
-        keys, vals = kv[step, 0], kv[step, 1]
-        q, g = q_ref[:, pair], g_ref[:, pair]
-        for h in range(2):
-            cols = slice(h * DH, (h + 1) * DH)
-            kx = jnp.concatenate([keys[:, cols], rsel[h]], 1)
-            qx = jnp.concatenate([q[:, cols], qr], 1)
-            gh = g[:, cols]
-            s = lax.dot_general(kx, qx, NT, preferred_element_type=F32)
-            s = jnp.concatenate([s[:PLEN], jnp.where(see, s[PLEN:], -1e30)], 0)
-            m = jnp.max(s, axis=0, keepdims=True)
-            p = jnp.exp2((s - m) * (SCALE * math.log2(math.e)))
-            p = p * (1.0 / jnp.sum(p, axis=0, keepdims=True))
-            pb = p.astype(BF16)
-            dprob = lax.dot_general(vals[:, cols], gh, NT, preferred_element_type=F32)
-            delta = jnp.sum(pb.astype(F32) * dprob, axis=0, keepdims=True)
-            ds = (p * (dprob - delta)).astype(BF16)
-            dk = jnp.dot(ds, qx, preferred_element_type=F32)
-            dkv[:, cols] = (dk[:, :DH] * SCALE).astype(BF16)
-            racc[h] += dk[:PLEN, DH:]
-            dkv[:, 256 + h * DH : 256 + (h + 1) * DH] = jnp.dot(pb, gh, preferred_element_type=F32).astype(BF16)
-        both = jnp.concatenate([wk_ref[:, pair], wv_ref[:, pair]], 1)
+    def weights_of(i):
+        part = jnp.dot(lat_t[...], dkv[...], preferred_element_type=F32).astype(BF16)
+        wpart[i] = part.reshape(2, 2, 4, 2, 16, 512)
+
+    def latents_of(i):
+        cols = pl.ds(pl.multiple_of(i * 256, 256), 256)
+        both = jnp.concatenate([wk_ref[:, cols], wv_ref[:, cols]], 1)
         lacc[...] += lax.dot_general(dkv[:PLEN], both, NT, preferred_element_type=F32)
 
-    @pl.when(step == PAIRS - 1)
-    def _():
-        lpart[:, :, :DC] = lacc[...].astype(BF16).reshape(8, 64, DC)
-        rope = (racc[0, :, :DR] + racc[1, :, DR:]) * SCALE
-        rope = jnp.concatenate([rope, jnp.zeros((PLEN, WIDE - DC - DR), F32)], 1)
-        lpart[:, :, DC:] = rope.astype(BF16).reshape(8, 64, WIDE - DC)
-        for b in range(1, 8):
-            remote(lpart.at[b], l1recv.at[b - 1], l1_send, l1_recv, at_xy(*OVER_XY[b])).start()
-
-    @pl.when((step >= 1) & (step < PAIRS + 1))
-    def _():
-        i = step - 1
+    def add_core(i):
         swap_core(i).wait()
         for lo in range(2):
             csum[i, lo] = (wpart[i, lo, core].astype(F32) + crecv[i, lo].astype(F32)).astype(BF16)
@@ -174,15 +148,7 @@
                 csum.at[i, to % 2, (y + dy) % 4, to // 2], drecv.at[i, n], d_send.at[i], d_recv.at[i], at_xy(dx, dy)
             ).start()
 
-    @pl.when(step < PAIRS)
-    def _():
-        part = jnp.dot(lat_t[...], dkv[...], preferred_element_type=F32).astype(BF16)
-        wpart[step] = part.reshape(2, 2, 4, 2, 16, 512)
-        swap_core(step).start()
-
-    @pl.when(step >= 2)
-    def _():
-        i = step - 2
+    def add_owned(i):
         arrived(drecv.at[i], d_recv.at[i])
         total = csum[i, x_lo, y, x_hi].astype(F32)
         for n in range(15):
@@ -192,28 +158,99 @@
         gw_ref[1, :, cols] = total[:, 256:]
         arrived(drecv.at[i], d_send.at[i])
 
-    @pl.when(step == PAIRS)
-    def _():
-        arrived(l1recv, l1_recv)
-        total = lpart[0].astype(F32)
+    before = jnp.maximum(step - 1, 0)
+    pair = pl.ds(pl.multiple_of(step * 256, 256), 256)
+    qr = qr_ref[:, pl.ds(pl.multiple_of(step * DH, DH), DH)]
+    see = lax.broadcasted_iota(jnp.int32, (CLEN, CLEN), 0) <= lax.broadcasted_iota(jnp.int32, (CLEN, CLEN), 1)
+    keys, vals = kv[step, 0], kv[step, 1]
+    q, g = q_ref[:, pair], g_ref[:, pair]
+    for h in range(2):
+        cols = slice(h * DH, (h + 1) * DH)
+        kx = jnp.concatenate([keys[:, cols], rsel[h]], 1)
+        qx = jnp.concatenate([q[:, cols], qr], 1)
+        gh = g[:, cols]
+        s = lax.dot_general(kx, qx, NT, preferred_element_type=F32)
+        s = jnp.concatenate([s[:PLEN], jnp.where(see, s[PLEN:], -1e30)], 0)
+        if h == 0:
+            weights_of(before)
+        else:
+            latents_of(before)
+        m = jnp.max(s, axis=0, keepdims=True)
+        p = jnp.exp2((s - m) * (SCALE * math.log2(math.e)))
+        p = p * (1.0 / jnp.sum(p, axis=0, keepdims=True))
+        pb = p.astype(BF16)
+        dprob = lax.dot_general(vals[:, cols], gh, NT, preferred_element_type=F32)
+        delta = jnp.sum(pb.astype(F32) * dprob, axis=0, keepdims=True)
+        ds = (p * (dprob - delta)).astype(BF16)
+        dk = jnp.dot(ds, qx, preferred_element_type=F32)
+        dkv_new[:, cols] = (dk[:, :DH] * SCALE).astype(BF16)
+        racc[h] += dk[:PLEN, DH:]
+        dkv_new[:, 256 + h * DH : 256 + (h + 1) * DH] = jnp.dot(pb, gh, preferred_element_type=F32).astype(BF16)
+    dkv[...] = dkv_new[...]
+
+    @pl.when(step >= 1)
+    def _():
+        swap_core(step - 1).start()
+
+    @pl.when((step >= 2) & (step < PAIRS - 1))
+    def _():
+        add_core(step - 2)
+
+    @pl.when((step >= 3) & (step < PAIRS - 1))
+    def _():
+        add_owned(step - 3)
+
+    @pl.when(step == PAIRS - 1)
+    def _():
+        last = PAIRS - 1
+        latents_of(last)
+        apart[...] = lacc[:, :ACOLS].astype(BF16).reshape(8, 64, ACOLS)
+        for b in range(1, 8):
+            remote(apart.at[b], a1recv.at[b - 1], a1_send, a1_recv, at_xy(*OVER_XY[b])).start()
+        rope = (racc[0, :, :DR] + racc[1, :, DR:]) * SCALE
+        rest = jnp.concatenate([lacc[:, ACOLS:], rope, jnp.zeros((PLEN, DH - DR), F32)], 1)
+        for k in range(8):
+            rows = jnp.concatenate([rest[b * 64 + k * 8 : b * 64 + k * 8 + 8] for b in range(8)], 0)
+            bpart[k] = rows.astype(BF16)
+        for k in range(1, 8):
+            remote(bpart.at[k], b1recv.at[k - 1], b1_send, b1_recv, at_z(OVER_Z[k])).start()
+        add_core(last - 2)
+        weights_of(last)
+        swap_core(last).start()
+        add_core(last - 1)
+        add_owned(last - 3)
+        add_core(last)
+        add_owned(last - 2)
+        arrived(a1recv, a1_recv)
+        total = apart[0].astype(F32)
         for b in range(7):
-            total = total + l1recv[b].astype(F32)
-        total = jnp.concatenate([total, jnp.zeros((64, 2 * PACK - WIDE), F32)], 1).reshape(8, 8, 2 * PACK)
-        total = jnp.concatenate([total[:, :, :PACK], total[:, :, PACK:]], 1)
-        l2own[...] = total[0]
-        l2src[...] = total.astype(BF16)
+            total = total + a1recv[b].astype(F32)
+        a2src[...] = total.reshape(8, 8, ACOLS)
         for k in range(1, 8):
-            remote(l2src.at[k], l2recv.at[k - 1], l2_send, l2_recv, at_z(OVER_Z[k])).start()
-
-    @pl.when(step == PAIRS + 1)
-    def _():
-        arrived(l2recv, l2_recv)
-        total = l2own[...]
+            remote(a2src.at[k], a2recv.at[k - 1], a2_send, a2_recv, at_z(OVER_Z[k])).start()
+        arrived(b1recv, b1_recv)
+        total = bpart[0].astype(F32)
         for k in range(7):
-            total = total + l2recv[k].astype(F32)
-        glat_ref[...] = jnp.concatenate([total[:8], total[8:, : WIDE - PACK]], 1)
-        arrived(l1recv, l1_send)
-        arrived(l2recv, l2_send)
+            total = total + b1recv[k].astype(F32)
+        b2src[...] = total.reshape(8, 8, BCOLS)
+        for b in range(1, 8):
+            remote(b2src.at[b], b2recv.at[b - 1], b2_send, b2_recv, at_xy(*OVER_XY[b])).start()
+        add_owned(last - 1)
+        add_owned(last)
+        arrived(a2recv, a2_recv)
+        total = a2src[0]
+        for k in range(7):
+            total = total + a2recv[k]
+        glat_ref[:, :ACOLS] = total
+        arrived(b2recv, b2_recv)
+        total = b2src[0]
+        for b in range(7):
+            total = total + b2recv[b]
+        glat_ref[:, ACOLS:] = total
+        arrived(a1recv, a1_send)
+        arrived(b1recv, b1_send)
+        arrived(a2recv, a2_send)
+        arrived(b2recv, b2_send)
 
 
 def finish(lat_ref, w_ref, glat_ref, grope_ref, gwk_ref, gwv_ref):
@@ -230,23 +267,24 @@
     vmem, dma = pltpu.VMEM, pltpu.SemaphoreType.DMA
     lat, weights = pl.pallas_call(
         kernel,
-        grid=(PAIRS + 2,),
-        in_specs=[pl.BlockSpec(memory_space=pltpu.SMEM)] + [pl.BlockSpec(memory_space=pl.ANY)] * 9,
+        grid=(PAIRS,),
+        in_specs=[pl.BlockSpec(memory_space=pl.ANY)] * 10,
         out_specs=[whole(8, WIDE), whole(2, 16, 2048)],
         out_shape=[jax.ShapeDtypeStruct((8, WIDE), F32), jax.ShapeDtypeStruct((2, 16, 2048), F32)],
         scratch_shapes=[
             vmem((8, DC), BF16), vmem((8, DR), BF16), vmem((CLEN, DC), BF16), vmem((DR, CLEN), BF16),
             vmem((CLEN, 2048), BF16), vmem((CLEN, 1024), BF16), vmem((CLEN, 2048), BF16),
-            vmem((DC, 2048), BF16), vmem((DC, 2048), BF16),
+            vmem((DC, 2048), BF16), vmem((DC, 2048), BF16), vmem((1, 1), jnp.int32),
             vmem((8, 16, PACK), BF16), vmem((12, 64, WIDE), BF16), vmem((DC, KEYS), BF16), vmem((2, KEYS, DH), BF16),
-            vmem((PAIRS, 2, KEYS, 256), BF16), vmem((KEYS, 512), BF16), vmem((PLEN, DC), F32), vmem((2, PLEN, DH), F32),
+            vmem((PAIRS, 2, KEYS, 256), BF16), vmem((KEYS, 512), BF16), vmem((KEYS, 512), BF16),
+            vmem((PLEN, DC), F32), vmem((2, PLEN, DH), F32),
             vmem((PAIRS, 2, 2, 4, 2, 16, 512), BF16),
             vmem((PAIRS, 2, 4, 2, 16, 512), BF16), vmem((PAIRS, 2, 4, 2, 16, 512), BF16),
             vmem((PAIRS, 15, 16, 512), BF16),
-            vmem((8, 64, WIDE), BF16), vmem((7, 64, WIDE), BF16),
-            vmem((8, 16, PACK), BF16), vmem((16, PACK), F32), vmem((7, 16, PACK), BF16),
-            dma((9,)), dma, dma, dma, dma((2,)), dma((PAIRS,)), dma((PAIRS,)), dma((PAIRS,)), dma((PAIRS,)),
-            dma, dma, dma, dma,
+            vmem((8, 64, ACOLS), BF16), vmem((7, 64, ACOLS), BF16), vmem((8, 8, ACOLS), F32), vmem((7, 8, ACOLS), F32),
+            vmem((8, 64, BCOLS), BF16), vmem((7, 64, BCOLS), BF16), vmem((8, 8, BCOLS), F32), vmem((7, 8, BCOLS), F32),
+            dma((10,)), dma, dma, dma, dma((2,)), dma((PAIRS,)), dma((PAIRS,)), dma((PAIRS,)), dma((PAIRS,)),
+            dma, dma, dma, dma, dma, dma, dma, dma,
         ],
         compiler_params=pltpu.CompilerParams(
             vmem_limit_bytes=56 * 1024 * 1024, collective_id=0, has_side_effects=True

time: 79.6 us -> 75.8 us (0.952)
  Pallas kernels: 76.9 us -> 73.7 us
    pallas_call x1, Pallas kernels: 75.2 us -> 72 us  [local(): pl.pallas_call(kernel, grid=(PAIRS,), in_specs=[pl.BlockSpec(memory_space...]
where the time goes in v3:
time: 75.8 us; the launch traced here: 75 us
  Pallas kernels  73.7 us (97%)
  between operations  1.29 us (2%)
    pallas_call x1, Pallas kernels, local(): pl.pallas_call(kernel, grid=(PAIRS,), in_specs=[pl.BlockSpec(memory_space...  72 us
    pallas_call x1, Pallas kernels, local(): pl.pallas_call(finish, out_shape=[jax.ShapeDtypeStruct((8, DC), F32), jax...  1.68 us

profile of v3, /device:TPU:2, one launch (start us, length us, event | category | flops | bytes accessed | tf_op | source)
XLA Modules:
  0.0 75.0 jit_solution(7061161167210029976)
XLA Ops:
  1.3 72.0 %mla_backward.1 = (f32[8,640]{1,0:T(8,128)}, f32[2,16,2048]{2,1,0:T(8,128)}) custom-call(s32[1,1]{1,0:T(1,128)S(6)} %copy.14.len_hbm, bf16[8,512]{1,0:T(8,128)(2,1)} %bitcast.17, bf16[8,64]{1,0:T(8,128)(2,1)} %bitcast.19, bf16[256,512]{1,0:T(8,128)(2,1)} %bitcast.14, bf16[64,256]{1,0:T(8,128)(2,1)} %bitcast.15, bf16[256,2048]{1,0:T(8,128)(2,1)} %bitcast.11, ...), custom_call_target="tpu_custom_call" | custom-call | flops 12999999488 | bytes 8000000 | tf_op jit(solution)/shard_map/mla_backward/pallas_call | solution.py:268
  73.3 1.7 %outputs.1 = (f32[8,512]{1,0:T(8,128)}, f32[8,64]{1,0:T(8,128)}, f32[16,2048]{1,0:T(8,128)}, f32[16,2048]{1,0:T(8,128)}) custom-call(f32[8,640]{1,0:T(8,128)} %get-tuple-element.10.lat_ref, f32[2,16,2048]{2,1,0:T(8,128)} %get-tuple-element.11.w_ref), custom_call_target="tpu_custom_call" | custom-call | tf_op jit(solution)/shard_map/outputs/pallas_call | solution.py:298

commit v4 on v3

--- a/solution.py
+++ b/solution.py
@@ -18,6 +18,7 @@
 BCOLS = WIDE - ACOLS
 PACK = 384
 PAIRS = 8
+LAG = 5
 NT = (((1,), (1,)), ((), ()))
 SCALE = 1.0 / (DH + DR) ** 0.5
 F32 = jnp.float32
@@ -66,15 +67,12 @@
     def project(first, count):
         rows = lat[first : first + count, :, :DC].reshape(count * 64, DC)
 
-        def pair(i, carry):
-            cols = pl.ds(pl.multiple_of(i * 256, 256), 256)
+        for i in range(PAIRS):
+            cols = slice(i * 256, (i + 1) * 256)
             for half, w in enumerate((wk_ref, wv_ref)):
                 kv[i, half, first * 64 : (first + count) * 64] = jnp.dot(
                     rows, w[:, cols], preferred_element_type=F32
                 ).astype(BF16)
-            return carry
-
-        lax.fori_loop(0, PAIRS, pair, 0)
         tokens = slice(first * 64, (first + count) * 64)
         lat_t[:, tokens] = rows.T
         rope = lat[first : first + count, :, DC:].reshape(count * 64, DH)
@@ -196,9 +194,9 @@
     def _():
         add_core(step - 2)
 
-    @pl.when((step >= 3) & (step < PAIRS - 1))
-    def _():
-        add_owned(step - 3)
+    @pl.when((step >= LAG) & (step < PAIRS - 1))
+    def _():
+        add_owned(step - LAG)
 
     @pl.when(step == PAIRS - 1)
     def _():
@@ -218,9 +216,10 @@
         weights_of(last)
         swap_core(last).start()
         add_core(last - 1)
+        for i in range(last - LAG, last - 3):
+            add_owned(i)
+        add_core(last)
         add_owned(last - 3)
-        add_core(last)
-        add_owned(last - 2)
         arrived(a1recv, a1_recv)
         total = apart[0].astype(F32)
         for b in range(7):
@@ -235,8 +234,8 @@
         b2src[...] = total.reshape(8, 8, BCOLS)
         for b in range(1, 8):
             remote(b2src.at[b], b2recv.at[b - 1], b2_send, b2_recv, at_xy(*OVER_XY[b])).start()
-        add_owned(last - 1)
-        add_owned(last)
+        for i in range(last - 2, last + 1):
+            add_owned(i)
         arrived(a2recv, a2_recv)
         total = a2src[0]
         for k in range(7):

time: 75.8 us -> 68.3 us (0.901)
  Pallas kernels: 73.7 us -> 66.3 us
    pallas_call x1, Pallas kernels: 72 us -> 64.6 us  [local(): pl.pallas_call(kernel, grid=(PAIRS,), in_specs=[pl.BlockSpec(memory_space...]
where the time goes in v4:
time: 68.3 us; the launch traced here: 67.5 us
  Pallas kernels  66.3 us (97%)
  between operations  1.29 us (2%)
    pallas_call x1, Pallas kernels, local(): pl.pallas_call(kernel, grid=(PAIRS,), in_specs=[pl.BlockSpec(memory_space...  64.6 us
    pallas_call x1, Pallas kernels, local(): pl.pallas_call(finish, out_shape=[jax.ShapeDtypeStruct((8, DC), F32), jax...  1.68 us

profile of v4, /device:TPU:2, one launch (start us, length us, event | category | flops | bytes accessed | tf_op | source)
XLA Modules:
  0.0 67.5 jit_solution(5300848192364205366)
XLA Ops:
  1.3 64.6 %mla_backward.1 = (f32[8,640]{1,0:T(8,128)}, f32[2,16,2048]{2,1,0:T(8,128)}) custom-call(s32[1,1]{1,0:T(1,128)S(6)} %copy.14.len_hbm, bf16[8,512]{1,0:T(8,128)(2,1)} %bitcast.17, bf16[8,64]{1,0:T(8,128)(2,1)} %bitcast.19, bf16[256,512]{1,0:T(8,128)(2,1)} %bitcast.14, bf16[64,256]{1,0:T(8,128)(2,1)} %bitcast.15, bf16[256,2048]{1,0:T(8,128)(2,1)} %bitcast.11, ...), custom_call_target="tpu_custom_call" | custom-call | flops 12999999488 | bytes 8000000 | tf_op jit(solution)/shard_map/mla_backward/pallas_call | solution.py:267
  65.9 1.7 %outputs.1 = (f32[8,512]{1,0:T(8,128)}, f32[8,64]{1,0:T(8,128)}, f32[16,2048]{1,0:T(8,128)}, f32[16,2048]{1,0:T(8,128)}) custom-call(f32[8,640]{1,0:T(8,128)} %get-tuple-element.10.lat_ref, f32[2,16,2048]{2,1,0:T(8,128)} %get-tuple-element.11.w_ref), custom_call_target="tpu_custom_call" | custom-call | tf_op jit(solution)/shard_map/outputs/pallas_call | solution.py:297

commit v5 on v4

--- a/solution.py
+++ b/solution.py
@@ -18,7 +18,7 @@
 BCOLS = WIDE - ACOLS
 PACK = 384
 PAIRS = 8
-LAG = 5
+STEPS = PAIRS // 2
 NT = (((1,), (1,)), ((), ()))
 SCALE = 1.0 / (DH + DR) ** 0.5
 F32 = jnp.float32
@@ -33,9 +33,10 @@
     len_hbm, plat_hbm, prope_hbm, clat_hbm, crope_hbm, q_hbm, qr_hbm, g_hbm, wk_hbm, wv_hbm,
     glat_ref, gw_ref,
     plat, prope, clat, crope, q_ref, qr_ref, g_ref, wk_ref, wv_ref, len_ref,
-    gz, lat, lat_t, rsel, kv, dkv, dkv_new, lacc, racc,
-    wpart, crecv, csum, drecv, apart, a1recv, a2src, a2recv, bpart, b1recv, b2src, b2recv,
-    load, gz_send, gz_recv, gy_send, gy_recv, c_send, c_recv, d_send, d_recv,
+    gz, gl, gr, lat, lat_t, rsel, kv, dkv_a, dkv_b, lacc, racc,
+    wpart, crecv, csum, krecv1, ksum, krecv2, vrecv1, vsum, vrecv2, apart, a1recv, a2src, a2recv, bpart, b1recv, b2src, b2recv,
+    load, gz_send, gz_recv, gl_send, gl_recv, gr_send, gr_recv, c_send, c_recv,
+    k1_send, k1_recv, k2_send, k2_recv, v1_send, v1_recv, v2_send, v2_recv,
     a1_send, a1_recv, a2_send, a2_recv, b1_send, b1_recv, b2_send, b2_recv,
 ):
     step = pl.program_id(0)
@@ -94,44 +95,75 @@
             pl.semaphore_signal(barrier, inc=1, device_id=peer, device_id_type=MESH)
         loads[0].wait()
         loads[1].wait()
-        wide = jnp.concatenate([plat[...].astype(F32), prope[...].astype(F32), jnp.zeros((8, 2 * PACK - DC - DR), F32)], 1)
-        gz[0] = jnp.concatenate([wide[:, :PACK], wide[:, PACK:]], 0).astype(BF16)
+        wide = plat[...].astype(F32)
+        rope = jnp.concatenate([prope[...].astype(F32), jnp.zeros((8, DH - DR), F32)], 1)
+        gz[0] = jnp.concatenate(
+            [jnp.concatenate([wide[:, :256], wide[:, 256:]], 0), jnp.concatenate([rope, jnp.zeros((8, DH), F32)], 0)], 1
+        ).astype(BF16)
         pl.semaphore_wait(barrier, len(peers))
         for k in range(1, 8):
-            remote(gz.at[0], gz.at[k], gz_send, gz_recv, at_z(8 - OVER_Z[k])).start()
+            remote(gz.at[0], gz.at[k], gz_send, gz_recv.at[k // 5], at_z(8 - OVER_Z[k])).start()
+
+        def forward(first, count):
+            for b in range(1, 8):
+                dx, dy = OVER_XY[b]
+                blocks = pl.ds(first, count)
+                remote(
+                    gz.at[blocks, :, pl.ds(0, 256)], gl.at[b, blocks], gl_send, gl_recv.at[b // 4], at_xy(4 - dx, 4 - dy)
+                ).start()
+
+        def unpack(first, count):
+            block = gl[first : first + count].astype(F32)
+            block = jnp.concatenate([block[:, :, :8], block[:, :, 8:]], 3)
+            lat[first : first + count, :, :DC] = block.reshape(count, 64, DC).astype(BF16)
+            for b in range(first, first + count):
+                rope = gr[b].astype(F32)
+                rope = jnp.concatenate([rope[:, :DR], rope[:, DR:]], 0)
+                lat[b, :, DC:] = jnp.concatenate([rope, jnp.zeros((64, DH - DR), F32)], 1).astype(BF16)
+
+        forward(0, 1)
         loads[2].wait()
         loads[3].wait()
         lat[8:12, :, :DC] = clat[...].reshape(4, 64, DC)
         rope = jnp.concatenate([crope[...].astype(F32).T, jnp.zeros((CLEN, WIDE - DC - DR), F32)], 1)
         lat[8:12, :, DC:] = rope.astype(BF16).reshape(4, 64, WIDE - DC)
-        dkv[...] = jnp.zeros_like(dkv)
-        lacc[...] = jnp.zeros_like(lacc)
-        racc[...] = jnp.zeros_like(racc)
         loads[4].wait()
         loads[5].wait()
         project(8, 4)
-        arrived(gz.at[pl.ds(1, 7)], gz_recv)
-        block = gz[...].astype(F32)
-        lat[0] = jnp.concatenate([block[:, :8], block[:, 8:, : WIDE - PACK]], 2).reshape(64, WIDE).astype(BF16)
+        arrived(gz.at[pl.ds(1, 4)], gz_recv.at[0])
+        forward(1, 4)
+        dkv_b[...] = jnp.zeros_like(dkv_b)
+        lacc[...] = jnp.zeros_like(lacc)
+        racc[...] = jnp.zeros_like(racc)
+        arrived(gz.at[pl.ds(5, 3)], gz_recv.at[1])
+        forward(5, 3)
+        rope = gz[:, :, 256:].astype(F32)[:, :8, :DR].reshape(64, DR)
+        gr[0] = jnp.concatenate([rope[:32], rope[32:]], 1).astype(BF16)
         for b in range(1, 8):
             dx, dy = OVER_XY[b]
-            remote(lat.at[0], lat.at[b], gy_send, gy_recv.at[b // 4], at_xy(4 - dx, 4 - dy)).start()
+            remote(gr.at[0], gr.at[b], gr_send, gr_recv.at[b // 4], at_xy(4 - dx, 4 - dy)).start()
+        gl[0] = gz[:, :, :256]
         for copy in loads[6:]:
             copy.wait()
         live = lax.broadcasted_iota(jnp.int32, g_ref.shape, 0) < len_ref[...]
         g_ref[...] = jnp.where(live, g_ref[...], jnp.zeros((), BF16))
-        arrived(lat.at[pl.ds(1, 3)], gy_recv.at[0])
+        arrived(gl.at[pl.ds(1, 3)], gl_recv.at[0])
+        arrived(gr.at[pl.ds(1, 3)], gr_recv.at[0])
+        unpack(0, 4)
         project(0, 4)
-        arrived(lat.at[pl.ds(4, 4)], gy_recv.at[1])
+        arrived(gl.at[pl.ds(4, 4)], gl_recv.at[1])
+        arrived(gr.at[pl.ds(4, 4)], gr_recv.at[1])
+        unpack(4, 4)
         project(4, 4)
         arrived(gz.at[pl.ds(1, 7)], gz_send)
-        arrived(lat.at[pl.ds(1, 7)], gy_send)
-
-    def weights_of(i):
+        arrived(gl.at[pl.ds(1, 7)], gl_send)
+        arrived(gr.at[pl.ds(1, 7)], gr_send)
+
+    def weights_of(i, dkv):
         part = jnp.dot(lat_t[...], dkv[...], preferred_element_type=F32).astype(BF16)
         wpart[i] = part.reshape(2, 2, 4, 2, 16, 512)
 
-    def latents_of(i):
+    def latents_of(i, dkv):
         cols = pl.ds(pl.multiple_of(i * 256, 256), 256)
         both = jnp.concatenate([wk_ref[:, cols], wv_ref[:, cols]], 1)
         lacc[...] += lax.dot_general(dkv[:PLEN], both, NT, preferred_element_type=F32)
@@ -139,69 +171,106 @@
     def add_core(i):
         swap_core(i).wait()
         for lo in range(2):
-            csum[i, lo] = (wpart[i, lo, core].astype(F32) + crecv[i, lo].astype(F32)).astype(BF16)
-        for n, (dx, dy) in enumerate(ALL_XY):
-            to = (x + dx) % 4
-            remote(
-                csum.at[i, to % 2, (y + dy) % 4, to // 2], drecv.at[i, n], d_send.at[i], d_recv.at[i], at_xy(dx, dy)
-            ).start()
+            total = wpart[i, lo, core].astype(F32) + crecv[i, lo].astype(F32)
+            csum[i, 0, lo] = total[..., :256].astype(BF16)
+            csum[i, 1, lo] = total[..., 256:].astype(BF16)
+        for d in (1, 2, 3):
+            to = (x + d) % 4
+            remote(csum.at[i, 0, to % 2, :, to // 2], krecv1.at[i, d - 1], k1_send.at[i], k1_recv.at[i], at_xy(d, 0)).start()
+            remote(csum.at[i, 1, :, (y + d) % 4], vrecv1.at[i, d - 1], v1_send.at[i], v1_recv.at[i], at_xy(0, d)).start()
+
+    def add_first(i):
+        arrived(krecv1.at[i], k1_recv.at[i])
+        arrived(vrecv1.at[i], v1_recv.at[i])
+        k = csum[i, 0, x_lo, :, x_hi].astype(F32)
+        v = csum[i, 1, :, y].astype(F32)
+        for d in range(3):
+            k = k + krecv1[i, d].astype(F32)
+            v = v + vrecv1[i, d].astype(F32)
+        ksum[i] = k.astype(BF16)
+        vsum[i] = v.astype(BF16)
+        for d in (1, 2, 3):
+            to = (x + d) % 4
+            remote(ksum.at[i, (y + d) % 4], krecv2.at[i, d - 1], k2_send.at[i], k2_recv.at[i], at_xy(0, d)).start()
+            remote(vsum.at[i, to % 2, to // 2], vrecv2.at[i, d - 1], v2_send.at[i], v2_recv.at[i], at_xy(d, 0)).start()
 
     def add_owned(i):
-        arrived(drecv.at[i], d_recv.at[i])
-        total = csum[i, x_lo, y, x_hi].astype(F32)
-        for n in range(15):
-            total = total + drecv[i, n].astype(F32)
+        arrived(krecv2.at[i], k2_recv.at[i])
+        arrived(vrecv2.at[i], v2_recv.at[i])
+        k = ksum[i, y].astype(F32)
+        v = vsum[i, x_lo, x_hi].astype(F32)
+        for d in range(3):
+            k = k + krecv2[i, d].astype(F32)
+            v = v + vrecv2[i, d].astype(F32)
         cols = pl.ds(pl.multiple_of(i * 256, 256), 256)
-        gw_ref[0, :, cols] = total[:, :256]
-        gw_ref[1, :, cols] = total[:, 256:]
-        arrived(drecv.at[i], d_send.at[i])
-
-    before = jnp.maximum(step - 1, 0)
-    pair = pl.ds(pl.multiple_of(step * 256, 256), 256)
-    qr = qr_ref[:, pl.ds(pl.multiple_of(step * DH, DH), DH)]
+        gw_ref[0, :, cols] = k
+        gw_ref[1, :, cols] = v
+        arrived(krecv1.at[i], k1_send.at[i])
+        arrived(vrecv1.at[i], v1_send.at[i])
+        arrived(krecv2.at[i], k2_send.at[i])
+        arrived(vrecv2.at[i], v2_send.at[i])
+
     see = lax.broadcasted_iota(jnp.int32, (CLEN, CLEN), 0) <= lax.broadcasted_iota(jnp.int32, (CLEN, CLEN), 1)
-    keys, vals = kv[step, 0], kv[step, 1]
-    q, g = q_ref[:, pair], g_ref[:, pair]
-    for h in range(2):
-        cols = slice(h * DH, (h + 1) * DH)
-        kx = jnp.concatenate([keys[:, cols], rsel[h]], 1)
-        qx = jnp.concatenate([q[:, cols], qr], 1)
-        gh = g[:, cols]
-        s = lax.dot_general(kx, qx, NT, preferred_element_type=F32)
-        s = jnp.concatenate([s[:PLEN], jnp.where(see, s[PLEN:], -1e30)], 0)
-        if h == 0:
-            weights_of(before)
-        else:
-            latents_of(before)
-        m = jnp.max(s, axis=0, keepdims=True)
-        p = jnp.exp2((s - m) * (SCALE * math.log2(math.e)))
-        p = p * (1.0 / jnp.sum(p, axis=0, keepdims=True))
-        pb = p.astype(BF16)
-        dprob = lax.dot_general(vals[:, cols], gh, NT, preferred_element_type=F32)
-        delta = jnp.sum(pb.astype(F32) * dprob, axis=0, keepdims=True)
-        ds = (p * (dprob - delta)).astype(BF16)
-        dk = jnp.dot(ds, qx, preferred_element_type=F32)
-        dkv_new[:, cols] = (dk[:, :DH] * SCALE).astype(BF16)
-        racc[h] += dk[:PLEN, DH:]
-        dkv_new[:, 256 + h * DH : 256 + (h + 1) * DH] = jnp.dot(pb, gh, preferred_element_type=F32).astype(BF16)
-    dkv[...] = dkv_new[...]
+
+    def attend(i, new, before, old):
+        pair = pl.ds(pl.multiple_of(i * 256, 256), 256)
+        qr = qr_ref[:, pl.ds(pl.multiple_of(i * DH, DH), DH)]
+        keys, vals = kv[i, 0], kv[i, 1]
+        q, g = q_ref[:, pair], g_ref[:, pair]
+        heads = []
+        for h in range(2):
+            cols = slice(h * DH, (h + 1) * DH)
+            kx = jnp.concatenate([keys[:, cols], rsel[h]], 1)
+            qx = jnp.concatenate([q[:, cols], qr], 1)
+            s = lax.dot_general(kx, qx, NT, preferred_element_type=F32)
+            dprob = lax.dot_general(vals[:, cols], g[:, cols], NT, preferred_element_type=F32)
+            heads.append((cols, qx, g[:, cols], s, dprob))
+        weights_of(before, old)
+        latents_of(before, old)
+        for h, (cols, qx, gh, s, dprob) in enumerate(heads):
+            s = jnp.concatenate([s[:PLEN], jnp.where(see, s[PLEN:], -1e30)], 0)
+            m = jnp.max(s, axis=0, keepdims=True)
+            p = jnp.exp2((s - m) * (SCALE * math.log2(math.e)))
+            p = p * (1.0 / jnp.sum(p, axis=0, keepdims=True))
+            pb = p.astype(BF16)
+            new[:, 256 + h * DH : 256 + (h + 1) * DH] = jnp.dot(pb, gh, preferred_element_type=F32).astype(BF16)
+            delta = jnp.sum(pb.astype(F32) * dprob, axis=0, keepdims=True)
+            ds = (p * (dprob - delta)).astype(BF16)
+            dk = jnp.dot(ds, qx, preferred_element_type=F32)
+            new[:, cols] = (dk[:, :DH] * SCALE).astype(BF16)
+            racc[h] += dk[:PLEN, DH:]
+
+    first, second = 2 * step, 2 * step + 1
+    attend(first, dkv_a, jnp.maximum(first - 1, 0), dkv_b)
 
     @pl.when(step >= 1)
     def _():
-        swap_core(step - 1).start()
-
-    @pl.when((step >= 2) & (step < PAIRS - 1))
-    def _():
-        add_core(step - 2)
-
-    @pl.when((step >= LAG) & (step < PAIRS - 1))
-    def _():
-        add_owned(step - LAG)
-
-    @pl.when(step == PAIRS - 1)
+        swap_core(first - 1).start()
+        add_core(first - 2)
+
+    @pl.when(step >= 2)
+    def _():
+        add_first(first - 4)
+
+    @pl.when(step >= 3)
+    def _():
+        add_owned(first - 6)
+
+    attend(second, dkv_b, first, dkv_a)
+    swap_core(first).start()
+
+    @pl.when((step >= 1) & (step < STEPS - 1))
+    def _():
+        add_core(first - 1)
+
+    @pl.when((step >= 2) & (step < STEPS - 1))
+    def _():
+        add_first(first - 3)
+
+    @pl.when(step == STEPS - 1)
     def _():
         last = PAIRS - 1
-        latents_of(last)
+        latents_of(last, dkv_b)
         apart[...] = lacc[:, :ACOLS].astype(BF16).reshape(8, 64, ACOLS)
         for b in range(1, 8):
             remote(apart.at[b], a1recv.at[b - 1], a1_send, a1_recv, at_xy(*OVER_XY[b])).start()
@@ -213,13 +282,16 @@
         for k in range(1, 8):
             remote(bpart.at[k], b1recv.at[k - 1], b1_send, b1_recv, at_z(OVER_Z[k])).start()
         add_core(last - 2)
-        weights_of(last)
+        weights_of(last, dkv_b)
         swap_core(last).start()
+        add_first(last - 4)
         add_core(last - 1)
-        for i in range(last - LAG, last - 3):
-            add_owned(i)
+        add_first(last - 3)
         add_core(last)
-        add_owned(last - 3)
+        add_owned(last - 6)
+        add_owned(last - 5)
+        add_first(last - 2)
+        add_first(last - 1)
         arrived(a1recv, a1_recv)
         total = apart[0].astype(F32)
         for b in range(7):
@@ -227,6 +299,7 @@
         a2src[...] = total.reshape(8, 8, ACOLS)
         for k in range(1, 8):
             remote(a2src.at[k], a2recv.at[k - 1], a2_send, a2_recv, at_z(OVER_Z[k])).start()
+        add_first(last)
         arrived(b1recv, b1_recv)
         total = bpart[0].astype(F32)
         for k in range(7):
@@ -234,7 +307,7 @@
         b2src[...] = total.reshape(8, 8, BCOLS)
         for b in range(1, 8):
             remote(b2src.at[b], b2recv.at[b - 1], b2_send, b2_recv, at_xy(*OVER_XY[b])).start()
-        for i in range(last - 2, last + 1):
+        for i in range(last - 4, last + 1):
             add_owned(i)
         arrived(a2recv, a2_recv)
         total = a2src[0]
@@ -266,7 +339,7 @@
     vmem, dma = pltpu.VMEM, pltpu.SemaphoreType.DMA
     lat, weights = pl.pallas_call(
         kernel,
-        grid=(PAIRS,),
+        grid=(STEPS,),
         in_specs=[pl.BlockSpec(memory_space=pl.ANY)] * 10,
         out_specs=[whole(8, WIDE), whole(2, 16, 2048)],
         out_shape=[jax.ShapeDtypeStruct((8, WIDE), F32), jax.ShapeDtypeStruct((2, 16, 2048), F32)],
@@ -274,16 +347,19 @@
             vmem((8, DC), BF16), vmem((8, DR), BF16), vmem((CLEN, DC), BF16), vmem((DR, CLEN), BF16),
             vmem((CLEN, 2048), BF16), vmem((CLEN, 1024), BF16), vmem((CLEN, 2048), BF16),
             vmem((DC, 2048), BF16), vmem((DC, 2048), BF16), vmem((1, 1), jnp.int32),
-            vmem((8, 16, PACK), BF16), vmem((12, 64, WIDE), BF16), vmem((DC, KEYS), BF16), vmem((2, KEYS, DH), BF16),
+            vmem((8, 16, PACK), BF16), vmem((8, 8, 16, 256), BF16), vmem((8, 32, DH), BF16),
+            vmem((12, 64, WIDE), BF16), vmem((DC, KEYS), BF16), vmem((2, KEYS, DH), BF16),
             vmem((PAIRS, 2, KEYS, 256), BF16), vmem((KEYS, 512), BF16), vmem((KEYS, 512), BF16),
             vmem((PLEN, DC), F32), vmem((2, PLEN, DH), F32),
             vmem((PAIRS, 2, 2, 4, 2, 16, 512), BF16),
-            vmem((PAIRS, 2, 4, 2, 16, 512), BF16), vmem((PAIRS, 2, 4, 2, 16, 512), BF16),
-            vmem((PAIRS, 15, 16, 512), BF16),
+            vmem((PAIRS, 2, 4, 2, 16, 512), BF16),
+            vmem((PAIRS, 2, 2, 4, 2, 16, 256), BF16),
+            vmem((PAIRS, 3, 4, 16, 256), BF16), vmem((PAIRS, 4, 16, 256), BF16), vmem((PAIRS, 3, 16, 256), BF16),
+            vmem((PAIRS, 3, 2, 2, 16, 256), BF16), vmem((PAIRS, 2, 2, 16, 256), BF16), vmem((PAIRS, 3, 16, 256), BF16),
             vmem((8, 64, ACOLS), BF16), vmem((7, 64, ACOLS), BF16), vmem((8, 8, ACOLS), F32), vmem((7, 8, ACOLS), F32),
             vmem((8, 64, BCOLS), BF16), vmem((7, 64, BCOLS), BF16), vmem((8, 8, BCOLS), F32), vmem((7, 8, BCOLS), F32),
-            dma((10,)), dma, dma, dma, dma((2,)), dma((PAIRS,)), dma((PAIRS,)), dma((PAIRS,)), dma((PAIRS,)),
-            dma, dma, dma, dma, dma, dma, dma, dma,
+            dma((10,)), dma, dma((2,)), dma, dma((2,)), dma, dma((2,)),
+            *[dma((PAIRS,))] * 10, *[dma] * 8,
         ],
         compiler_params=pltpu.CompilerParams(
             vmem_limit_bytes=56 * 1024 * 1024, collective_id=0, has_side_effects=True

time: 68.3 us -> 62.7 us (0.918)
  Pallas kernels: 66.3 us -> 60.9 us
    pallas_call x1, Pallas kernels: 64.6 us -> 59.2 us  [local(): pl.pallas_call(kernel, grid=(STEPS,), in_specs=[pl.BlockSpec(memory_space...]
where the time goes in v5:
time: 62.7 us; the launch traced here: 62.2 us
  Pallas kernels  60.9 us (97%)
  between operations  1.29 us (2%)
    pallas_call x1, Pallas kernels, local(): pl.pallas_call(kernel, grid=(STEPS,), in_specs=[pl.BlockSpec(memory_space...  59.2 us
    pallas_call x1, Pallas kernels, local(): pl.pallas_call(finish, out_shape=[jax.ShapeDtypeStruct((8, DC), F32), jax...  1.68 us

profile of v5, /device:TPU:2, one launch (start us, length us, event | category | flops | bytes accessed | tf_op | source)
XLA Modules:
  0.0 62.2 jit_solution(5286760105930448759)
XLA Ops:
  1.3 59.2 %mla_backward.1 = (f32[8,640]{1,0:T(8,128)}, f32[2,16,2048]{2,1,0:T(8,128)}) custom-call(s32[1,1]{1,0:T(1,128)S(6)} %copy.14.len_hbm, bf16[8,512]{1,0:T(8,128)(2,1)} %bitcast.17, bf16[8,64]{1,0:T(8,128)(2,1)} %bitcast.19, bf16[256,512]{1,0:T(8,128)(2,1)} %bitcast.14, bf16[64,256]{1,0:T(8,128)(2,1)} %bitcast.15, bf16[256,2048]{1,0:T(8,128)(2,1)} %bitcast.11, ...), custom_call_target="tpu_custom_call" | custom-call | flops 12999999488 | bytes 8000000 | tf_op jit(solution)/shard_map/mla_backward/pallas_call | solution.py:340
  60.5 1.7 %outputs.1 = (f32[8,512]{1,0:T(8,128)}, f32[8,64]{1,0:T(8,128)}, f32[16,2048]{1,0:T(8,128)}, f32[16,2048]{1,0:T(8,128)}) custom-call(f32[8,640]{1,0:T(8,128)} %get-tuple-element.10.lat_ref, f32[2,16,2048]{2,1,0:T(8,128)} %get-tuple-element.11.w_ref), custom_call_target="tpu_custom_call" | custom-call | tf_op jit(solution)/shard_map/outputs/pallas_call | solution.py:373

commit v6 on v5

--- a/solution.py
+++ b/solution.py
@@ -34,23 +34,23 @@
     glat_ref, gw_ref,
     plat, prope, clat, crope, q_ref, qr_ref, g_ref, wk_ref, wv_ref, len_ref,
     gz, gl, gr, lat, lat_t, rsel, kv, dkv_a, dkv_b, lacc, racc,
-    wpart, crecv, csum, krecv1, ksum, krecv2, vrecv1, vsum, vrecv2, apart, a1recv, a2src, a2recv, bpart, b1recv, b2src, b2recv,
+    wpart, crecv, csum, krecv1, ksum, krecv2, vrecv1, vsum, vrecv2, apart, a1recv, a2src, a2own, a2recv, bpart, b1recv, b2src, b2recv,
     load, gz_send, gz_recv, gl_send, gl_recv, gr_send, gr_recv, c_send, c_recv,
     k1_send, k1_recv, k2_send, k2_recv, v1_send, v1_recv, v2_send, v2_recv,
     a1_send, a1_recv, a2_send, a2_recv, b1_send, b1_recv, b2_send, b2_recv,
 ):
     step = pl.program_id(0)
     dp, sample, z = lax.axis_index("dp"), lax.axis_index("sample"), lax.axis_index("head")
-    x_lo, core = dp // 2, dp % 2
-    y, x_hi = sample // 2, sample % 2
+    x_lo, core = lax.div(dp, 2), lax.rem(dp, 2)
+    y, x_hi = lax.div(sample, 2), lax.rem(sample, 2)
     x = x_hi * 2 + x_lo
 
     def at_xy(dx, dy):
-        to = (x + dx) % 4
-        return {"dp": (to % 2) * 2 + core, "sample": ((y + dy) % 4) * 2 + to // 2}
+        to = lax.rem(x + dx, 4)
+        return {"dp": lax.rem(to, 2) * 2 + core, "sample": lax.rem(y + dy, 4) * 2 + lax.div(to, 2)}
 
     def at_z(d):
-        return {"head": (z + d) % 8}
+        return {"head": lax.rem(z + d, 8)}
 
     other_core = {"dp": x_lo * 2 + 1 - core}
 
@@ -175,9 +175,9 @@
             csum[i, 0, lo] = total[..., :256].astype(BF16)
             csum[i, 1, lo] = total[..., 256:].astype(BF16)
         for d in (1, 2, 3):
-            to = (x + d) % 4
-            remote(csum.at[i, 0, to % 2, :, to // 2], krecv1.at[i, d - 1], k1_send.at[i], k1_recv.at[i], at_xy(d, 0)).start()
-            remote(csum.at[i, 1, :, (y + d) % 4], vrecv1.at[i, d - 1], v1_send.at[i], v1_recv.at[i], at_xy(0, d)).start()
+            to = lax.rem(x + d, 4)
+            remote(csum.at[i, 0, lax.rem(to, 2), :, lax.div(to, 2)], krecv1.at[i, d - 1], k1_send.at[i], k1_recv.at[i], at_xy(d, 0)).start()
+            remote(csum.at[i, 1, :, lax.rem(y + d, 4)], vrecv1.at[i, d - 1], v1_send.at[i], v1_recv.at[i], at_xy(0, d)).start()
 
     def add_first(i):
         arrived(krecv1.at[i], k1_recv.at[i])
@@ -190,9 +190,9 @@
         ksum[i] = k.astype(BF16)
         vsum[i] = v.astype(BF16)
         for d in (1, 2, 3):
-            to = (x + d) % 4
-            remote(ksum.at[i, (y + d) % 4], krecv2.at[i, d - 1], k2_send.at[i], k2_recv.at[i], at_xy(0, d)).start()
-            remote(vsum.at[i, to % 2, to // 2], vrecv2.at[i, d - 1], v2_send.at[i], v2_recv.at[i], at_xy(d, 0)).start()
+            to = lax.rem(x + d, 4)
+            remote(ksum.at[i, lax.rem(y + d, 4)], krecv2.at[i, d - 1], k2_send.at[i], k2_recv.at[i], at_xy(0, d)).start()
+            remote(vsum.at[i, lax.rem(to, 2), lax.div(to, 2)], vrecv2.at[i, d - 1], v2_send.at[i], v2_recv.at[i], at_xy(d, 0)).start()
 
     def add_owned(i):
         arrived(krecv2.at[i], k2_recv.at[i])
@@ -212,33 +212,53 @@
 
     see = lax.broadcasted_iota(jnp.int32, (CLEN, CLEN), 0) <= lax.broadcasted_iota(jnp.int32, (CLEN, CLEN), 1)
 
+    last = PAIRS - 1
+
+    def scores(i, h):
+        start = pl.multiple_of(i * 256, 256) + h * DH
+        mine = pl.ds(pl.multiple_of(start, DH), DH)
+        cols = slice(h * DH, (h + 1) * DH)
+        kx = jnp.concatenate([kv[i, 0, :, cols], rsel[h]], 1)
+        qx = jnp.concatenate([q_ref[:, mine], qr_ref[:, pl.ds(pl.multiple_of(i * DH, DH), DH)]], 1)
+        g = g_ref[:, mine]
+        s = lax.dot_general(kx, qx, NT, preferred_element_type=F32)
+        dprob = lax.dot_general(kv[i, 1, :, cols], g, NT, preferred_element_type=F32)
+        return qx, g, s, dprob
+
+    def gradients(h, new, qx, g, s, dprob):
+        s = jnp.concatenate([s[:PLEN], jnp.where(see, s[PLEN:], -1e30)], 0)
+        m = jnp.max(s, axis=0, keepdims=True)
+        p = jnp.exp2((s - m) * (SCALE * math.log2(math.e)))
+        p = p * (1.0 / jnp.sum(p, axis=0, keepdims=True))
+        pb = p.astype(BF16)
+        new[:, 256 + h * DH : 256 + (h + 1) * DH] = jnp.dot(pb, g, preferred_element_type=F32).astype(BF16)
+        delta = jnp.sum(pb.astype(F32) * dprob, axis=0, keepdims=True)
+        ds = (p * (dprob - delta)).astype(BF16)
+        dk = jnp.dot(ds, qx, preferred_element_type=F32)
+        new[:, h * DH : (h + 1) * DH] = (dk[:, :DH] * SCALE).astype(BF16)
+        racc[h] += dk[:PLEN, DH:]
+
     def attend(i, new, before, old):
-        pair = pl.ds(pl.multiple_of(i * 256, 256), 256)
-        qr = qr_ref[:, pl.ds(pl.multiple_of(i * DH, DH), DH)]
-        keys, vals = kv[i, 0], kv[i, 1]
-        q, g = q_ref[:, pair], g_ref[:, pair]
-        heads = []
-        for h in range(2):
-            cols = slice(h * DH, (h + 1) * DH)
-            kx = jnp.concatenate([keys[:, cols], rsel[h]], 1)
-            qx = jnp.concatenate([q[:, cols], qr], 1)
-            s = lax.dot_general(kx, qx, NT, preferred_element_type=F32)
-            dprob = lax.dot_general(vals[:, cols], g[:, cols], NT, preferred_element_type=F32)
-            heads.append((cols, qx, g[:, cols], s, dprob))
+        one = scores(i, 0)
         weights_of(before, old)
+        two = scores(i, 1)
         latents_of(before, old)
-        for h, (cols, qx, gh, s, dprob) in enumerate(heads):
-            s = jnp.concatenate([s[:PLEN], jnp.where(see, s[PLEN:], -1e30)], 0)
-            m = jnp.max(s, axis=0, keepdims=True)
-            p = jnp.exp2((s - m) * (SCALE * math.log2(math.e)))
-            p = p * (1.0 / jnp.sum(p, axis=0, keepdims=True))
-            pb = p.astype(BF16)
-            new[:, 256 + h * DH : 256 + (h + 1) * DH] = jnp.dot(pb, gh, preferred_element_type=F32).astype(BF16)
-            delta = jnp.sum(pb.astype(F32) * dprob, axis=0, keepdims=True)
-            ds = (p * (dprob - delta)).astype(BF16)
-            dk = jnp.dot(ds, qx, preferred_element_type=F32)
-            new[:, cols] = (dk[:, :DH] * SCALE).astype(BF16)
-            racc[h] += dk[:PLEN, DH:]
+        gradients(0, new, *one)
+        gradients(1, new, *two)
+
+    def grads_of_head(h):
+        return jnp.concatenate([dkv_b[:, h * DH : (h + 1) * DH], dkv_b[:, 256 + h * DH : 256 + (h + 1) * DH]], 1)
+
+    def weights_of_head(h):
+        part = jnp.dot(lat_t[...], grads_of_head(h), preferred_element_type=F32).astype(BF16)
+        for n in range(2):
+            cols = slice(n * 256 + h * DH, n * 256 + (h + 1) * DH)
+            wpart[last, :, :, :, :, :, cols] = part[:, n * DH : (n + 1) * DH].reshape(2, 2, 4, 2, 16, DH)
+
+    def latents_of_head(h):
+        mine = slice(last * 256 + h * DH, last * 256 + (h + 1) * DH)
+        both = jnp.concatenate([wk_ref[:, mine], wv_ref[:, mine]], 1)
+        lacc[...] += lax.dot_general(grads_of_head(h)[:PLEN], both, NT, preferred_element_type=F32)
 
     first, second = 2 * step, 2 * step + 1
     attend(first, dkv_a, jnp.maximum(first - 1, 0), dkv_b)
@@ -256,8 +276,10 @@
     def _():
         add_owned(first - 6)
 
-    attend(second, dkv_b, first, dkv_a)
-    swap_core(first).start()
+    @pl.when(step < STEPS - 1)
+    def _():
+        attend(second, dkv_b, first, dkv_a)
+        swap_core(first).start()
 
     @pl.when((step >= 1) & (step < STEPS - 1))
     def _():
@@ -269,25 +291,42 @@
 
     @pl.when(step == STEPS - 1)
     def _():
-        last = PAIRS - 1
-        latents_of(last, dkv_b)
+        head = scores(last, 0)
+        weights_of(last - 1, dkv_a)
+        latents_of(last - 1, dkv_a)
+        gradients(0, dkv_b, *head)
+        swap_core(last - 1).start()
+        add_core(last - 2)
+        add_first(last - 4)
+
+    @pl.when(step == STEPS - 1)
+    def _():
+        head = scores(last, 1)
+        weights_of_head(0)
+        latents_of_head(0)
+        gradients(1, dkv_b, *head)
+
+    @pl.when(step == STEPS - 1)
+    def _():
+        latents_of_head(1)
         apart[...] = lacc[:, :ACOLS].astype(BF16).reshape(8, 64, ACOLS)
         for b in range(1, 8):
             remote(apart.at[b], a1recv.at[b - 1], a1_send, a1_recv, at_xy(*OVER_XY[b])).start()
+        weights_of_head(1)
+        swap_core(last).start()
+        add_core(last - 1)
         rope = (racc[0, :, :DR] + racc[1, :, DR:]) * SCALE
-        rest = jnp.concatenate([lacc[:, ACOLS:], rope, jnp.zeros((PLEN, DH - DR), F32)], 1)
+        rest = lacc[:, ACOLS:]
         for k in range(8):
-            rows = jnp.concatenate([rest[b * 64 + k * 8 : b * 64 + k * 8 + 8] for b in range(8)], 0)
-            bpart[k] = rows.astype(BF16)
+            mine = [slice(b * 64 + k * 8, b * 64 + k * 8 + 8) for b in range(8)]
+            left = jnp.concatenate([rope[rows] for rows in mine[:4]], 0)
+            right = jnp.concatenate([rope[rows] for rows in mine[4:]], 0)
+            both = jnp.concatenate([left, right], 1)
+            bpart[k] = jnp.concatenate([rest[rows] for rows in mine] + [both], 0).astype(BF16)
         for k in range(1, 8):
             remote(bpart.at[k], b1recv.at[k - 1], b1_send, b1_recv, at_z(OVER_Z[k])).start()
-        add_core(last - 2)
-        weights_of(last, dkv_b)
-        swap_core(last).start()
-        add_first(last - 4)
-        add_core(last - 1)
+        add_core(last)
         add_first(last - 3)
-        add_core(last)
         add_owned(last - 6)
         add_owned(last - 5)
         add_first(last - 2)
@@ -296,7 +335,10 @@
         total = apart[0].astype(F32)
         for b in range(7):
             total = total + a1recv[b].astype(F32)
-        a2src[...] = total.reshape(8, 8, ACOLS)
+        total = total.reshape(8, 8, ACOLS)
+        a2own[...] = total[0]
+        right = jnp.concatenate([total[:, :, 256:], jnp.zeros((8, 8, 512 - ACOLS), F32)], 2)
+        a2src[...] = jnp.concatenate([total[:, :, :256], right], 1).astype(BF16)
         for k in range(1, 8):
             remote(a2src.at[k], a2recv.at[k - 1], a2_send, a2_recv, at_z(OVER_Z[k])).start()
         add_first(last)
@@ -304,16 +346,19 @@
         total = bpart[0].astype(F32)
         for k in range(7):
             total = total + b1recv[k].astype(F32)
-        b2src[...] = total.reshape(8, 8, BCOLS)
+        rope = jnp.concatenate([total[64:, :DR], total[64:, DR:]], 0)
+        rope = jnp.concatenate([rope, jnp.zeros((64, DH - DR), F32)], 1)
+        b2src[...] = jnp.concatenate([total[:64], rope], 1).reshape(8, 8, BCOLS)
         for b in range(1, 8):
             remote(b2src.at[b], b2recv.at[b - 1], b2_send, b2_recv, at_xy(*OVER_XY[b])).start()
         for i in range(last - 4, last + 1):
             add_owned(i)
         arrived(a2recv, a2_recv)
-        total = a2src[0]
-        for k in range(7):
-            total = total + a2recv[k]
-        glat_ref[:, :ACOLS] = total
+        total = a2recv[0].astype(F32)
+        for k in range(1, 7):
+            total = total + a2recv[k].astype(F32)
+        glat_ref[:, :256] = a2own[:, :256] + total[:8]
+        glat_ref[:, 256:ACOLS] = a2own[:, 256:] + total[8:, : ACOLS - 256]
         arrived(b2recv, b2_recv)
         total = b2src[0]
         for b in range(7):
@@ -356,8 +401,8 @@
             vmem((PAIRS, 2, 2, 4, 2, 16, 256), BF16),
             vmem((PAIRS, 3, 4, 16, 256), BF16), vmem((PAIRS, 4, 16, 256), BF16), vmem((PAIRS, 3, 16, 256), BF16),
             vmem((PAIRS, 3, 2, 2, 16, 256), BF16), vmem((PAIRS, 2, 2, 16, 256), BF16), vmem((PAIRS, 3, 16, 256), BF16),
-            vmem((8, 64, ACOLS), BF16), vmem((7, 64, ACOLS), BF16), vmem((8, 8, ACOLS), F32), vmem((7, 8, ACOLS), F32),
-            vmem((8, 64, BCOLS), BF16), vmem((7, 64, BCOLS), BF16), vmem((8, 8, BCOLS), F32), vmem((7, 8, BCOLS), F32),
+            vmem((8, 64, ACOLS), BF16), vmem((7, 64, ACOLS), BF16), vmem((8, 16, 256), BF16), vmem((8, ACOLS), F32), vmem((7, 16, 256), BF16),
+            vmem((8, 96, DH), BF16), vmem((7, 96, DH), BF16), vmem((8, 8, BCOLS), F32), vmem((7, 8, BCOLS), F32),
             dma((10,)), dma, dma((2,)), dma, dma((2,)), dma, dma((2,)),
             *[dma((PAIRS,))] * 10, *[dma] * 8,
         ],

time: 62.7 us -> 61.6 us (0.982)
  Pallas kernels: 60.9 us -> 59.9 us
    pallas_call x1, Pallas kernels: 59.2 us -> 58.2 us  [local(): pl.pallas_call(kernel, grid=(STEPS,), in_specs=[pl.BlockSpec(memory_space...]
where the time goes in v6:
time: 61.6 us; the launch traced here: 61.2 us
  Pallas kernels  59.9 us (97%)
  between operations  1.29 us (2%)
    pallas_call x1, Pallas kernels, local(): pl.pallas_call(kernel, grid=(STEPS,), in_specs=[pl.BlockSpec(memory_space...  58.2 us
    pallas_call x1, Pallas kernels, local(): pl.pallas_call(finish, out_shape=[jax.ShapeDtypeStruct((8, DC), F32), jax...  1.68 us

profile of v6, /device:TPU:2, one launch (start us, length us, event | category | flops | bytes accessed | tf_op | source)
XLA Modules:
  0.0 61.2 jit_solution(7962436299809704407)
XLA Ops:
  1.3 58.2 %mla_backward.1 = (f32[8,640]{1,0:T(8,128)}, f32[2,16,2048]{2,1,0:T(8,128)}) custom-call(s32[1,1]{1,0:T(1,128)S(6)} %copy.14.len_hbm, bf16[8,512]{1,0:T(8,128)(2,1)} %bitcast.17, bf16[8,64]{1,0:T(8,128)(2,1)} %bitcast.19, bf16[256,512]{1,0:T(8,128)(2,1)} %bitcast.14, bf16[64,256]{1,0:T(8,128)(2,1)} %bitcast.15, bf16[256,2048]{1,0:T(8,128)(2,1)} %bitcast.11, ...), custom_call_target="tpu_custom_call" | custom-call | flops 12999999488 | bytes 8000000 | tf_op jit(solution)/shard_map/mla_backward/pallas_call | solution.py:385
  59.5 1.7 %outputs.1 = (f32[8,512]{1,0:T(8,128)}, f32[8,64]{1,0:T(8,128)}, f32[16,2048]{1,0:T(8,128)}, f32[16,2048]{1,0:T(8,128)}) custom-call(f32[8,640]{1,0:T(8,128)} %get-tuple-element.10.lat_ref, f32[2,16,2048]{2,1,0:T(8,128)} %get-tuple-element.11.w_ref), custom_call_target="tpu_custom_call" | custom-call | tf_op jit(solution)/shard_map/outputs/pallas_call | solution.py:418

commit v7 on v6

--- a/solution.py
+++ b/solution.py
@@ -65,17 +65,18 @@
     def swap_core(i):
         return remote(wpart.at[i, :, 1 - core], crecv.at[i], c_send.at[i], c_recv.at[i], other_core)
 
-    def project(first, count):
+    def project(first, count, pairs=range(PAIRS)):
         rows = lat[first : first + count, :, :DC].reshape(count * 64, DC)
-
-        for i in range(PAIRS):
+        for i in pairs:
             cols = slice(i * 256, (i + 1) * 256)
             for half, w in enumerate((wk_ref, wv_ref)):
                 kv[i, half, first * 64 : (first + count) * 64] = jnp.dot(
                     rows, w[:, cols], preferred_element_type=F32
                 ).astype(BF16)
+
+    def place(first, count):
         tokens = slice(first * 64, (first + count) * 64)
-        lat_t[:, tokens] = rows.T
+        lat_t[:, tokens] = lat[first : first + count, :, :DC].reshape(count * 64, DC).T
         rope = lat[first : first + count, :, DC:].reshape(count * 64, DH)
         rsel[0, tokens] = rope
         rsel[1, tokens] = jnp.concatenate([jnp.zeros((count * 64, DR), BF16), rope[:, :DR]], 1)
@@ -130,9 +131,9 @@
         loads[4].wait()
         loads[5].wait()
         project(8, 4)
+        place(8, 4)
         arrived(gz.at[pl.ds(1, 4)], gz_recv.at[0])
         forward(1, 4)
-        dkv_b[...] = jnp.zeros_like(dkv_b)
         lacc[...] = jnp.zeros_like(lacc)
         racc[...] = jnp.zeros_like(racc)
         arrived(gz.at[pl.ds(5, 3)], gz_recv.at[1])
@@ -151,10 +152,12 @@
         arrived(gr.at[pl.ds(1, 3)], gr_recv.at[0])
         unpack(0, 4)
         project(0, 4)
+        place(0, 4)
         arrived(gl.at[pl.ds(4, 4)], gl_recv.at[1])
         arrived(gr.at[pl.ds(4, 4)], gr_recv.at[1])
         unpack(4, 4)
-        project(4, 4)
+        project(4, 4, (0,))
+        place(4, 4)
         arrived(gz.at[pl.ds(1, 7)], gz_send)
         arrived(gl.at[pl.ds(1, 7)], gl_send)
         arrived(gr.at[pl.ds(1, 7)], gr_send)
@@ -215,8 +218,7 @@
     last = PAIRS - 1
 
     def scores(i, h):
-        start = pl.multiple_of(i * 256, 256) + h * DH
-        mine = pl.ds(pl.multiple_of(start, DH), DH)
+        mine = pl.ds(pl.multiple_of(i * 256 + h * DH, DH), DH)
         cols = slice(h * DH, (h + 1) * DH)
         kx = jnp.concatenate([kv[i, 0, :, cols], rsel[h]], 1)
         qx = jnp.concatenate([q_ref[:, mine], qr_ref[:, pl.ds(pl.multiple_of(i * DH, DH), DH)]], 1)
@@ -261,10 +263,18 @@
         lacc[...] += lax.dot_general(grads_of_head(h)[:PLEN], both, NT, preferred_element_type=F32)
 
     first, second = 2 * step, 2 * step + 1
-    attend(first, dkv_a, jnp.maximum(first - 1, 0), dkv_b)
+
+    @pl.when(step == 0)
+    def _():
+        one = scores(0, 0)
+        two = scores(0, 1)
+        project(4, 4, range(1, PAIRS))
+        gradients(0, dkv_a, *one)
+        gradients(1, dkv_a, *two)
 
     @pl.when(step >= 1)
     def _():
+        attend(first, dkv_a, first - 1, dkv_b)
         swap_core(first - 1).start()
         add_core(first - 2)
 
@@ -330,7 +340,6 @@
         add_owned(last - 6)
         add_owned(last - 5)
         add_first(last - 2)
-        add_first(last - 1)
         arrived(a1recv, a1_recv)
         total = apart[0].astype(F32)
         for b in range(7):
@@ -341,6 +350,7 @@
         a2src[...] = jnp.concatenate([total[:, :, :256], right], 1).astype(BF16)
         for k in range(1, 8):
             remote(a2src.at[k], a2recv.at[k - 1], a2_send, a2_recv, at_z(OVER_Z[k])).start()
+        add_first(last - 1)
         add_first(last)
         arrived(b1recv, b1_recv)
         total = bpart[0].astype(F32)
@@ -351,8 +361,7 @@
         b2src[...] = jnp.concatenate([total[:64], rope], 1).reshape(8, 8, BCOLS)
         for b in range(1, 8):
             remote(b2src.at[b], b2recv.at[b - 1], b2_send, b2_recv, at_xy(*OVER_XY[b])).start()
-        for i in range(last - 4, last + 1):
-            add_owned(i)
+        lax.fori_loop(last - 4, last + 1, lambda i, c: (add_owned(i), c)[1], 0)
         arrived(a2recv, a2_recv)
         total = a2recv[0].astype(F32)
         for k in range(1, 7):

time: 61.6 us -> 61 us (level)
  no operation moved by 1% of the time
where the time goes in v7:
time: 61 us; the launch traced here: 60.6 us
  Pallas kernels  59.3 us (97%)
  between operations  1.29 us (2%)
    pallas_call x1, Pallas kernels, local(): pl.pallas_call(kernel, grid=(STEPS,), in_specs=[pl.BlockSpec(memory_space...  57.6 us
    pallas_call x1, Pallas kernels, local(): pl.pallas_call(finish, out_shape=[jax.ShapeDtypeStruct((8, DC), F32), jax...  1.68 us

profile of v7, /device:TPU:2, one launch (start us, length us, event | category | flops | bytes accessed | tf_op | source)
XLA Modules:
  0.0 60.6 jit_solution(6740647438219460092)
XLA Ops:
  1.3 57.6 %mla_backward.1 = (f32[8,640]{1,0:T(8,128)}, f32[2,16,2048]{2,1,0:T(8,128)}) custom-call(s32[1,1]{1,0:T(1,128)S(6)} %copy.14.len_hbm, bf16[8,512]{1,0:T(8,128)(2,1)} %bitcast.17, bf16[8,64]{1,0:T(8,128)(2,1)} %bitcast.19, bf16[256,512]{1,0:T(8,128)(2,1)} %bitcast.14, bf16[64,256]{1,0:T(8,128)(2,1)} %bitcast.15, bf16[256,2048]{1,0:T(8,128)(2,1)} %bitcast.11, ...), custom_call_target="tpu_custom_call" | custom-call | flops 12999999488 | bytes 8000000 | tf_op jit(solution)/shard_map/mla_backward/pallas_call | solution.py:394
  58.9 1.7 %outputs.1 = (f32[8,512]{1,0:T(8,128)}, f32[8,64]{1,0:T(8,128)}, f32[16,2048]{1,0:T(8,128)}, f32[16,2048]{1,0:T(8,128)}) custom-call(f32[8,640]{1,0:T(8,128)} %get-tuple-element.10.lat_ref, f32[2,16,2048]{2,1,0:T(8,128)} %get-tuple-element.11.w_ref), custom_call_target="tpu_custom_call" | custom-call | tf_op jit(solution)/shard_map/outputs/pallas_call | solution.py:427

commit v8 on v7

--- a/solution.py
+++ b/solution.py
@@ -102,7 +102,7 @@
             [jnp.concatenate([wide[:, :256], wide[:, 256:]], 0), jnp.concatenate([rope, jnp.zeros((8, DH), F32)], 0)], 1
         ).astype(BF16)
         pl.semaphore_wait(barrier, len(peers))
-        for k in range(1, 8):
+        for k in range(7, 0, -1):
             remote(gz.at[0], gz.at[k], gz_send, gz_recv.at[k // 5], at_z(8 - OVER_Z[k])).start()
 
         def forward(first, count):
@@ -333,7 +333,7 @@
             right = jnp.concatenate([rope[rows] for rows in mine[4:]], 0)
             both = jnp.concatenate([left, right], 1)
             bpart[k] = jnp.concatenate([rest[rows] for rows in mine] + [both], 0).astype(BF16)
-        for k in range(1, 8):
+        for k in range(7, 0, -1):
             remote(bpart.at[k], b1recv.at[k - 1], b1_send, b1_recv, at_z(OVER_Z[k])).start()
         add_core(last)
         add_first(last - 3)
@@ -348,7 +348,7 @@
         a2own[...] = total[0]
         right = jnp.concatenate([total[:, :, 256:], jnp.zeros((8, 8, 512 - ACOLS), F32)], 2)
         a2src[...] = jnp.concatenate([total[:, :, :256], right], 1).astype(BF16)
-        for k in range(1, 8):
+        for k in range(7, 0, -1):
             remote(a2src.at[k], a2recv.at[k - 1], a2_send, a2_recv, at_z(OVER_Z[k])).start()
         add_first(last - 1)
         add_first(last)

time: 61 us -> 61.2 us (level)
  no operation moved by 1% of the time
where the time goes in v8:
time: 61.2 us; the launch traced here: 60.6 us
  Pallas kernels  59.3 us (97%)
  between operations  1.29 us (2%)
    pallas_call x1, Pallas kernels, local(): pl.pallas_call(kernel, grid=(STEPS,), in_specs=[pl.BlockSpec(memory_space...  57.6 us
    pallas_call x1, Pallas kernels, local(): pl.pallas_call(finish, out_shape=[jax.ShapeDtypeStruct((8, DC), F32), jax...  1.68 us

profile of v8, /device:TPU:2, one launch (start us, length us, event | category | flops | bytes accessed | tf_op | source)
XLA Modules:
  0.0 60.6 jit_solution(1129897070334457683)
XLA Ops:
  1.3 57.6 %mla_backward.1 = (f32[8,640]{1,0:T(8,128)}, f32[2,16,2048]{2,1,0:T(8,128)}) custom-call(s32[1,1]{1,0:T(1,128)S(6)} %copy.14.len_hbm, bf16[8,512]{1,0:T(8,128)(2,1)} %bitcast.17, bf16[8,64]{1,0:T(8,128)(2,1)} %bitcast.19, bf16[256,512]{1,0:T(8,128)(2,1)} %bitcast.14, bf16[64,256]{1,0:T(8,128)(2,1)} %bitcast.15, bf16[256,2048]{1,0:T(8,128)(2,1)} %bitcast.11, ...), custom_call_target="tpu_custom_call" | custom-call | flops 12999999488 | bytes 8000000 | tf_op jit(solution)/shard_map/mla_backward/pallas_call | solution.py:394
  58.9 1.7 %outputs.1 = (f32[8,512]{1,0:T(8,128)}, f32[8,64]{1,0:T(8,128)}, f32[16,2048]{1,0:T(8,128)}, f32[16,2048]{1,0:T(8,128)}) custom-call(f32[8,640]{1,0:T(8,128)} %get-tuple-element.10.lat_ref, f32[2,16,2048]{2,1,0:T(8,128)} %get-tuple-element.11.w_ref), custom_call_target="tpu_custom_call" | custom-call | tf_op jit(solution)/shard_map/outputs/pallas_call | solution.py:427
